TPU v7x, 256 devices: a whole 4x4x8 slice. The times are simulated.
256 devices in a mesh: ctx: 128 (over z, y_lo, x, core), dp: 2 (over y_hi).
Axes of the slice: x: 4, y: 4 (y_hi: 2, y_lo: 2; y = y_hi * 2 + y_lo), z: 8, core: 2. Of those that a mesh axis runs over, the one named last changes fastest.
Arguments:
- hidden_in: bfloat16 [65536, 8192], P(('dp', 'ctx')), parts along dimension 0, may hold values from -32 to 32
- segment_ids: int32 [65536], P('dp'), parts along dimension 0, may hold values from 1023 to 32767, as said below
- w_query: bfloat16 [8192, 512], P('ctx'), may hold values from -0.0625 to 0.0625
- w_key: bfloat16 [8192, 128], P('ctx'), may hold values from -0.0625 to 0.0625
- w_value: bfloat16 [8192, 128], P('ctx'), may hold values from -0.0625 to 0.0625
- w_out: bfloat16 [512, 8192], P(None, 'ctx'), may hold values from -0.25 to 0.25
Outputs:
- attended: bfloat16 [65536, 8192], P(('dp', 'ctx')), parts along dimension 0
There are 2 independent parts, one for each index of `dp`. A program takes and returns all parts, laid end to end along the dimension named above; an argument that names none is the same for every part. Nothing has to cross between parts.
Inputs may be any that keep to these rules, and one draw needn't show every extreme that they name: `segment_ids`: A token's id is the position in sequence order of the last token of its document, so ids never fall along the sequence and tokens share an id exactly when they share a document; every document holds 1 to 1024 tokens, and the first one exactly 1024. Stored in the same block order as hidden_in.
All inputs are finite; a program needn't handle non-finite values.
Results may differ from a plain program's by a relative error of at most 0.034.
Values may be sent and summed in bfloat16 or wider, within the bound.
A program may use at most 128 MiB of HBM per device.

v0:
```python
import math

import jax
import jax.numpy as jnp
from jax import lax
from jax.sharding import PartitionSpec as P

REACH = 8


ROPE_BASE = 500000.0


def passed_along(value, axis, steps):
    count = lax.axis_size(axis)
    leading, last = (max(0, -steps), min(count, count - steps))
    return lax.ppermute(value, axis, [(source, source + steps) for source in range(leading, last)])


def rotate(rows_in, positions):
    half_dim = rows_in.shape[-1] // 2
    frequency = ROPE_BASE ** (-(jnp.arange(half_dim, dtype=jnp.float32) * 2.0) / rows_in.shape[-1])
    angles = positions.astype(jnp.float32)[:, None] * frequency[None, :]
    cosine = jnp.cos(angles)[:, None, :]
    sine_part = jnp.sin(angles)[:, None, :]
    front_part = rows_in[..., :half_dim]
    back_part = rows_in[..., half_dim:]
    return jnp.concatenate(
        [front_part * cosine - back_part * sine_part, back_part * cosine + front_part * sine_part],
        axis=-1,
    )


def storage_block(seq_block, cycle_size):
    return jnp.where(
        seq_block < cycle_size, 2 * seq_block, 2 * (2 * cycle_size - 1 - seq_block) + 1
    )


def window_meta(last_block, block_len, seg_blocks, cycle_size):
    blocks_in = last_block - REACH + jnp.arange(REACH + 1, dtype=jnp.int32)
    inside = blocks_in >= 0
    seg_rows = seg_blocks[storage_block(jnp.maximum(blocks_in, 0), cycle_size)]
    key_seg = jnp.where(inside[:, None], seg_rows, -1).reshape(-1)
    key_pos = (
        blocks_in[:, None] * block_len + jnp.arange(block_len, dtype=jnp.int32)[None, :]
    ).reshape(-1)
    return (key_seg, key_pos)


def attend(query_part, window, query_pos, key_pos, query_seg, key_seg, head_dim):
    key_part = window[:, :head_dim]
    value_part = window[:, head_dim:]
    scores = jnp.einsum(
        "qhd,kd->hqk", query_part, key_part, preferred_element_type=jnp.float32
    ) / math.sqrt(head_dim)
    allowed = (query_seg[:, None] == key_seg[None, :]) & (key_pos[None, :] <= query_pos[:, None])
    scores = jnp.where(allowed[None], scores, -1e30)
    row_peak = jnp.max(scores, axis=-1, keepdims=True)
    exp_terms = jnp.exp(scores - row_peak)
    weights = (exp_terms / jnp.sum(exp_terms, axis=-1, keepdims=True)).astype(jnp.bfloat16)
    mixed_part = jnp.einsum("hqk,kd->qhd", weights, value_part, preferred_element_type=jnp.float32)
    return mixed_part.reshape(mixed_part.shape[0], -1).astype(jnp.bfloat16)


def on_device(hidden_in, segment_ids, w_query, w_key, w_value, w_out):
    cycle_size = lax.axis_size("ctx")
    my_index = lax.axis_index("ctx")
    block_len = hidden_in.shape[0] // 2
    query_width = w_query.shape[1]
    head_dim = w_key.shape[1]
    head_count = query_width // head_dim
    row_count = hidden_in.shape[0]
    portions = (
        lax.all_gather(w_query, "ctx", axis=0, tiled=True),
        lax.all_gather(w_key, "ctx", axis=0, tiled=True),
        lax.all_gather(w_value, "ctx", axis=0, tiled=True),
    )
    query_sum, key_sum, value_sum = tuple(
        (jnp.dot(hidden_in, portion, preferred_element_type=jnp.float32) for portion in portions)
    )
    late_block = 2 * cycle_size - 1 - my_index
    offsets = jnp.arange(block_len, dtype=jnp.int32)
    own_pos = jnp.concatenate([my_index * block_len + offsets, late_block * block_len + offsets])
    queries = rotate(query_sum.reshape(row_count, head_count, head_dim), own_pos).astype(
        jnp.bfloat16
    )
    key_rows = (
        rotate(key_sum.reshape(row_count, 1, head_dim), own_pos)
        .reshape(row_count, head_dim)
        .astype(jnp.bfloat16)
    )
    value_rows = value_sum.astype(jnp.bfloat16)
    joined_kv = jnp.concatenate([key_rows, value_rows], axis=1)
    early_list = [joined_kv[:block_len]]
    late_list = [joined_kv[block_len:]]
    at_top = my_index == cycle_size - 1
    for repeat_index in range(REACH):
        from_below = passed_along(early_list[-1], "ctx", 1)
        from_above = passed_along(late_list[-1], "ctx", -1)
        late_list.append(jnp.where(at_top, early_list[-1], from_above))
        early_list.append(from_below)
    early_window = jnp.concatenate(early_list[::-1], axis=0)
    late_window = jnp.concatenate(late_list[::-1], axis=0)
    seg_blocks = segment_ids.reshape(2 * cycle_size, block_len)
    early_seg, early_pos = window_meta(my_index, block_len, seg_blocks, cycle_size)
    late_seg, late_pos = window_meta(late_block, block_len, seg_blocks, cycle_size)
    early_out = attend(
        queries[:block_len],
        early_window,
        own_pos[:block_len],
        early_pos,
        seg_blocks[2 * my_index],
        early_seg,
        head_dim,
    )
    late_out = attend(
        queries[block_len:],
        late_window,
        own_pos[block_len:],
        late_pos,
        seg_blocks[2 * my_index + 1],
        late_seg,
        head_dim,
    )
    mixed_rows = jnp.concatenate([early_out, late_out], axis=0)
    result = jnp.dot(
        mixed_rows,
        lax.all_gather(w_out, "ctx", axis=1, tiled=True),
        preferred_element_type=jnp.float32,
    )
    return result.astype(jnp.bfloat16)


def solution(mesh):
    in_specs = (
        P(("dp", "ctx"), None),
        P("dp"),
        P("ctx", None),
        P("ctx", None),
        P("ctx", None),
        P(None, "ctx"),
    )
    out_specs = P(("dp", "ctx"), None)
    return jax.shard_map(
        on_device, mesh=mesh, in_specs=in_specs, out_specs=out_specs, check_vma=False
    )
```

profile of v0, /device:TPU:9, one launch (start us, length us, event | category | flops | bytes accessed | tf_op | source)
XLA Modules:
  0.0 894.5 jit_solution(16290772834346905860)
XLA Ops:
  9.4 213.4 %all-gather.5.cloned.1.call-done = bf16[8192,128]{1,0:T(8,128)(2,1)} async-done(((bf16[64,128]{1,0:T(8,128)(2,1)}), bf16[8192,128]{1,0:T(8,128)(2,1)}) %all-gather.5.cloned.1.call-update) | async-done | bytes 2097168 | tf_op jit(solution)/shard_map/all_gather | solution.py:76
  222.8 4.4 convolution_bitcast_fusion
  227.5 209.5 %all-gather.7.cloned.1.call-done = bf16[8192,128]{1,0:T(8,128)(2,1)} async-done(((bf16[64,128]{1,0:T(8,128)(2,1)}), bf16[8192,128]{1,0:T(8,128)(2,1)}) %all-gather.7.cloned.1.call-update) | async-done | bytes 2097168 | tf_op jit(solution)/shard_map/all_gather | solution.py:77
  437.0 4.4 convolution_convert_fusion.1
  441.4 3.0 collective-permute-start.8
  444.5 3.1 collective-permute-done.8
  450.8 4.3 collective-permute-start.1
  455.1 3.1 collective-permute-done.1
  461.1 4.8 collective-permute-done.2
  467.8 5.8 collective-permute-done.3
  475.6 5.7 collective-permute-done.4
  483.2 5.7 collective-permute-done.5
  491.7 5.0 collective-permute-done.6
  499.1 7.0 collective-permute-start.9
  507.0 6.8 collective-permute-start.10
  514.7 6.9 collective-permute-start.11
  522.4 6.9 collective-permute-start.12
  530.2 6.9 collective-permute-start.13
  538.0 6.9 collective-permute-start.14
  545.7 7.0 collective-permute-start.15
  553.6 104.9 %all-gather.9.cloned.1.call-done = bf16[8192,512]{1,0:T(8,128)(2,1)} async-done(((bf16[64,512]{1,0:T(8,128)(2,1)}), bf16[8192,512]{1,0:T(8,128)(2,1)}) %all-gather.9.cloned.1.call-update) | async-done | bytes 8388624 | tf_op jit(solution)/shard_map/all_gather | solution.py:75
  658.5 7.0 fusion.62
  670.8 209.4 %all-gather.11.cloned.1.call-done = bf16[512,8192]{0,1:T(8,128)(2,1)} async-done(((bf16[512,64]{0,1:T(8,128)(2,1)}), bf16[512,8192]{0,1:T(8,128)(2,1)}) %all-gather.11.cloned.1.call-update) | async-done | bytes 8388624 | tf_op jit(solution)/shard_map/all_gather | solution.py:129
  880.2 7.8 convolution_convert_fusion
  (81 shorter events, 31.6 us)
Async XLA Ops:
  6.5 216.2 %all-gather.5.cloned.1.call-start = ((), (), s32[]{:S(2)}) async-start(), calls=%async_computation | async-start | bytes 2113536 | tf_op jit(solution)/shard_map/all_gather | solution.py:76
  7.3 429.7 %all-gather.7.cloned.1.call-start = ((), (), s32[]{:S(2)}) async-start(), calls=%async_computation.1 | async-start | bytes 2113536 | tf_op jit(solution)/shard_map/all_gather | solution.py:77
  8.0 650.5 %all-gather.9.cloned.1.call-start = ((), (), s32[]{:S(2)}) async-start(), calls=%async_computation.2 | async-start | bytes 8454144 | tf_op jit(solution)/shard_map/all_gather | solution.py:75
  8.7 871.4 %all-gather.11.cloned.1.call-start = ((), (), s32[]{:S(2)}) async-start(), calls=%async_computation.3 | async-start | bytes 8454144 | tf_op jit(solution)/shard_map/all_gather | solution.py:129
  227.5 222.1 %copy-start = (s32[32768]{0:T(1024)S(1)}, s32[32768]{0:T(1024)}, u32[]{:S(2)}) copy-start(s32[32768]{0:T(1024)} %param.7) | copy-start | bytes 393220
  441.4 6.2 collective-permute-start.8
  447.6 3.2 collective-permute-start
  450.8 7.4 collective-permute-start.1
  458.2 7.7 collective-permute-start.2
  465.9 7.7 collective-permute-start.3
  473.6 7.7 collective-permute-start.4
  481.3 7.7 collective-permute-start.5
  488.9 7.7 collective-permute-start.6
  496.6 9.5 %collective-permute-start.7 = (bf16[128,256]{0,1:T(8,128)(2,1)S(1)}, bf16[128,256]{0,1:T(8,128)(2,1)S(1)}, u32[]{:S(2)}, u32[]{:S(2)}) collective-permute-start(bf16[128,256]{0,1:T(8,128)(2,1)S(1)} %collective-permute-done.6), channel_id=1, source_target_pairs={{0,2},{2,4},{4,6},{6,8},{8,10},{10,12},{12,14},{14,16},{16,18},{18... | collective-permute-start | bytes 196616 | tf_op jit(solution)/shard_map/ppermute | solution.py:17
  499.1 7.8 collective-permute-start.9
  507.0 7.6 collective-permute-start.10
  514.7 7.8 collective-permute-start.11
  522.4 7.8 collective-permute-start.12
  530.2 7.7 collective-permute-start.13
  538.0 7.7 collective-permute-start.14
  545.7 7.7 collective-permute-start.15
Sparse Core Ops, SparseCore 0:
  9.2 213.4 all-gather.4
  224.6 212.3 all-gather.6
  438.9 219.6 all-gather.8
  660.3 219.8 all-gather.10
where the time goes:
time: 898 us; the launch traced here: 895 us
  waiting for transfers between devices  778 us (87%)
  starting transfers between devices  69.8 us (8%)
  matrix products  28 us (3%)
  between operations  13.6 us (2%)
    all_gather x1, waiting for transfers between devices, on_device(): lax.all_gather(w_key, 'ctx', axis=0, tiled=True)  213 us
    all_gather x1, waiting for transfers between devices, on_device(): lax.all_gather(w_value, 'ctx', axis=0, tiled=True)  210 us
    all_gather x1, waiting for transfers between devices, on_device(): lax.all_gather(w_out, 'ctx', axis=1, tiled=True)  209 us
    all_gather x1, waiting for transfers between devices, on_device(): lax.all_gather(w_query, 'ctx', axis=0, tiled=True)  105 us
    ppermute x16, starting transfers between devices, passed_along(): lax.ppermute(value, axis, [(source, source + steps) for source in range(l...  69.7 us
    ppermute x16, waiting for transfers between devices, passed_along(): lax.ppermute(value, axis, [(source, source + steps) for source in range(l...  38.2 us
  transfers between devices with their start and end apart: 20, of which 19 were waited for; matrix products, arithmetic and copies ran while one was open for 3% of the time, Pallas kernels for 0%

commit v1 on v0

v1 whole, which is shorter than its diff:
```python
import functools
import math

import jax
import jax.numpy as jnp
import numpy as np
from jax import lax
from jax.experimental import pallas as pl
from jax.experimental.pallas import tpu as pltpu
from jax.sharding import PartitionSpec as P

MESH = pl.DeviceIdType.MESH
REACH = 8
ROPE_BASE = 500000.0
NZ, NY, NX = 8, 2, 4
CHIPS = NZ * NY * NX
BLOCK = 128
HD = 128
HQ = 4
D = 8192
QW = HQ * HD
QKV = QW + 2 * HD
SHARD = 64
ORDER = (0, 1, -1, 2, -2, 3, -3, 4)
FAR = -1e30
W_ROWS = ((0, 384), (384, 128))


class Gather:
    def __init__(self, place, ssem, rsem, sib_s, sib_r, slot, plane):
        self.place, self.ssem, self.rsem = place, ssem, rsem
        self.sib_s, self.sib_r = sib_s, sib_r
        self.slot, self.plane = slot, plane
        self.keys = ({}, {})
        self.sent = ([], [])

    def sem(self, core, key):
        table = self.keys[core]
        return table.setdefault(key, len(table))

    def send(self, core, where, key, move):
        index = self.sem(core, key)

        def make():
            ref = self.slot(core, *where)
            return pltpu.make_async_remote_copy(
                src_ref=ref, dst_ref=ref, send_sem=self.ssem.at[index], recv_sem=self.rsem.at[index],
                device_id=self.place.at(*move), device_id_type=MESH)

        make().start()
        self.sent[core].append(make)

    def recv(self, core, where, key):
        index = self.sem(core, key)
        ref = self.slot(core, *where)
        pltpu.make_async_remote_copy(
            src_ref=ref, dst_ref=ref, send_sem=self.ssem.at[index], recv_sem=self.rsem.at[index],
            device_id=self.place.sibling(), device_id_type=MESH).wait_recv()

    def sib_copy(self, core, zr):
        ref = self.plane(core, zr)
        index = (zr + NZ) % NZ
        return pltpu.make_async_remote_copy(
            src_ref=ref, dst_ref=ref, send_sem=self.sib_s.at[index], recv_sem=self.sib_r.at[index],
            device_id=self.place.sibling(), device_id_type=MESH)

    def sib(self, core, *planes):
        for zr in planes:
            self.sib_copy(core, zr).start()

    def drain(self, core):
        for make in self.sent[core]:
            make().wait_send()
        for zr in ORDER:
            self.sib_copy(core, zr).wait_send()

    def a_start(self):
        for step in (1, -1, 2):
            self.send(0, (0, 0, 0, None), ("X", step), (0, 0, step))

    def a_stream(self, j):
        xr = (0, -1, 1, 2)[j]
        if j:
            self.recv(0, (0, 0, xr, None), ("X", -xr if j < 3 else 2))
        for way in (1, -1):
            self.send(0, (0, 0, xr, None), ("Z", j, way, 1), (way, 0, 0))

    def a_y(self, *planes):
        for zr in planes:
            for way in (1, -1):
                self.send(0, (zr, 0, None, (1 - way) // 2), ("Y", zr, way), (0, way, 0))

    def a_step(self, s):
        for j in range(4):
            xr = (0, -1, 1, 2)[j]
            for way in (1, -1):
                half = (1 - way) // 2
                if s < 4:
                    self.recv(0, (-way * s, 0, xr, None), ("Z", j, way, s))
                    onward = half if s == 3 else None
                    self.send(0, (-way * s, 0, xr, onward), ("Z", j, way, s + 1), (way, 0, 0))
                else:
                    self.recv(0, (4, 0, xr, half), ("Z", j, way, 4))
        self.a_y(*((4,) if s == 4 else (-s, s)))

    def a_done(self, *planes):
        for zr in planes:
            for way in (1, -1):
                self.recv(0, (zr, 1, None, (1 - way) // 2), ("Y", zr, way))
        self.sib(0, *planes)

    def b_x(self, zr, yr):
        for way in (1, -1):
            self.send(1, (zr, yr, 0, None), ("X", zr, yr, way), (0, 0, way))

    def b_y(self, zr):
        for way in (1, -1):
            self.send(1, (zr, 0, 0, (1 - way) // 2), ("Y", zr, way), (0, way, 0))

    def b_start_z(self):
        for far in (1, 2, 3):
            for way in (1, -1):
                self.send(1, (0, 0, 0, None), ("Z", way, far), (way * far, 0, 0))

    def b_z(self, *planes, x=True):
        for zr in planes:
            if zr == 4:
                for way in (1, -1):
                    self.recv(1, (4, 0, 0, (1 - way) // 2), ("Z", way, 4))
            else:
                way = -1 if zr > 0 else 1
                self.recv(1, (zr, 0, 0, None), ("Z", way, abs(zr)))
                if abs(zr) == 3:
                    self.send(1, (zr, 0, 0, (1 - way) // 2), ("Z", way, 4), (way, 0, 0))
            if x:
                self.b_x(zr, 0)
            self.b_y(zr)

    def b_ywait(self, *planes, x=True):
        for zr in planes:
            for way in (1, -1):
                self.recv(1, (zr, 1, 0, (1 - way) // 2), ("Y", zr, way))
            if x:
                self.b_x(zr, 1)

    def b_relay(self, yr, *planes):
        for zr in planes:
            for way in (1, -1):
                self.recv(1, (zr, yr, -way, None), ("X", zr, yr, way))
                self.send(1, (zr, yr, -way, (1 - way) // 2), ("XR", zr, yr, way), (0, 0, way))

    def b_done(self, *planes):
        for zr in planes:
            for yr in (0, 1):
                for way in (1, -1):
                    self.recv(1, (zr, yr, 2, (1 - way) // 2), ("XR", zr, yr, way))
        self.sib(1, *planes)


class Place:
    def __init__(self):
        ctx, dp = lax.axis_index("ctx"), lax.axis_index("dp")
        self.ctx, self.dp = ctx, dp
        self.c = ctx % 2
        self.k = ctx // 2
        self.x = self.k % NX
        self.yl = (self.k // NX) % NY
        self.z = self.k // (NX * NY)
        self.y = dp * 2 + self.yl

    def zi(self, zr):
        return (self.z + (zr + NZ)) % NZ

    def yi(self, yr):
        return (self.yl + yr) % NY

    def xi(self, xr):
        return (self.x + (xr + NX)) % NX

    def at(self, dz, dy, dx):
        y = (self.y + (dy + 4)) % 4
        chip = (self.zi(dz) * NY + y % 2) * NX + self.xi(dx)
        return {"ctx": chip * 2 + self.c, "dp": y // 2}

    def sibling(self):
        return {"ctx": self.k * 2 + (1 - self.c), "dp": self.dp}

    def on(self, chip, core):
        return {"ctx": chip * 2 + core, "dp": self.dp}


def kernel(hid_hbm, seg_hbm, wq_hbm, wk_hbm, wv_hbm, wo_hbm, freq_ref, out_hbm,
           hid, seg, qbuf, wbuf, wo_in, wo_sib, acc, cos_t, sin_t, bias, qrot, kvw, mixed, outv,
           load_sem, out_sem, wo_s, wo_r, q_s, q_r, qs_s, qs_r, w_s, w_r, ws_s, ws_r,
           kv_s, kv_r, kvs_s, kvs_r):
    me = Place()
    c, k, i = me.c, me.k, me.ctx

    def q_slot(core, zr, yr, xr, half):
        rows = pl.ds(0, SHARD) if half is None else pl.ds(half * 32, 32)
        x = slice(None) if xr is None else me.xi(xr)
        return qbuf.at[me.zi(zr), me.yi(yr), x, core, rows, :]

    def q_plane(core, zr):
        return qbuf.at[me.zi(zr), :, :, core]

    def w_slot(core, zr, yr, xr, half):
        first, count = W_ROWS[core]
        rows = pl.ds(first, count) if half is None else pl.ds(first + half * (count // 2), count // 2)
        x = slice(None) if xr is None else me.xi(xr)
        return wbuf.at[me.zi(zr), me.yi(yr), x, rows, :]

    def w_plane(core, zr):
        return wbuf.at[me.zi(zr), :, :, pl.ds(*W_ROWS[core]), :]

    gq = Gather(me, q_s, q_r, qs_s, qs_r, q_slot, q_plane)
    gw = Gather(me, w_s, w_r, ws_s, ws_r, w_slot, w_plane)

    def both(first, second):
        pl.when(c == 0)(first)
        pl.when(c == 1)(second)

    own = qbuf.at[me.z, me.yl, me.x, c]
    loads = [
        pltpu.make_async_copy(wq_hbm, own.at[:, pl.ds(0, QW)], load_sem.at[0]),
        pltpu.make_async_copy(wk_hbm, own.at[:, pl.ds(QW, HD)], load_sem.at[1]),
        pltpu.make_async_copy(wv_hbm, own.at[:, pl.ds(QW + HD, HD)], load_sem.at[2]),
        pltpu.make_async_copy(wo_hbm, wo_in, load_sem.at[3]),
        pltpu.make_async_copy(seg_hbm, seg, load_sem.at[4]),
        pltpu.make_async_copy(hid_hbm, hid, load_sem.at[5]),
    ]
    for load in loads:
        load.start()

    kvw[0, 0:REACH] = jnp.zeros((REACH, BLOCK, 2 * HD), jnp.bfloat16)

    def up(m):
        over = k + m >= CHIPS
        return (jnp.where(over, 2 * CHIPS - 1 - k - m, k + m), jnp.where(over, 1 - c, c))

    barrier = pltpu.get_barrier_semaphore()

    def greet(device):
        pl.semaphore_signal(barrier, inc=1, device_id=device, device_id_type=MESH)

    moves = [(0, 0, 1), (0, 0, -1), (0, 0, 2), (0, 1, 0), (0, -1, 0)]
    moves += [(way * far, 0, 0) for far in (1, 2, 3) for way in (1, -1)]
    for move in moves:
        greet(me.at(*move))
    greet(me.sibling())
    for m in range(1, 5):
        greet(me.on(*up(m)))
        pl.when(k >= m)(lambda m=m: greet(me.on(k - m, c)))
    pl.semaphore_wait(barrier, len(moves) + 5 + jnp.minimum(k, 4))

    for load in loads[:3]:
        load.wait()

    def b_begin():
        gq.b_x(0, 0)
        gq.b_start_z()
        gq.b_y(0)

    def a_begin():
        gq.a_start()
        gq.a_stream(0)

    both(a_begin, b_begin)

    loads[3].wait()
    wo_copy = pltpu.make_async_remote_copy(
        src_ref=wo_in, dst_ref=wo_sib, send_sem=wo_s, recv_sem=wo_r,
        device_id=me.sibling(), device_id_type=MESH)
    wo_copy.start()

    row = lax.broadcasted_iota(jnp.int32, (BLOCK, HD), 0)
    lane = lax.broadcasted_iota(jnp.int32, (BLOCK, HD), 1)
    late = 2 * 2 * CHIPS - 1 - i
    for b, block in enumerate((i, late)):
        angle = (block * BLOCK + row).astype(jnp.float32) * freq_ref[...]
        cos_t[b] = jnp.cos(angle)
        sine = jnp.sin(angle)
        sin_t[b] = jnp.where(lane < HD // 2, -sine, sine)

    wo_copy.wait()

    def join(core):
        rows = pl.ds(*W_ROWS[core])
        pair = [wo_in[rows, :], wo_sib[rows, :]]
        wbuf[me.z, me.yl, me.x, rows, :] = jnp.concatenate(pair if core == 0 else pair[::-1], axis=1)

    def a1():
        for j in (1, 2, 3):
            gq.a_stream(j)
        gq.a_y(0)
        join(0)
        gw.a_start()

    def b1():
        gq.b_z(1, -1)
        gq.b_ywait(0)
        join(1)

    both(a1, b1)

    loads[4].wait()
    for b in range(2):
        mine = seg[pl.ds(2 * i + b, 1), :]
        asks = jnp.transpose(jnp.broadcast_to(mine, (BLOCK, BLOCK)))
        for j in range(REACH + 1):
            if b == 0:
                block = i - REACH + j
                keys = seg[pl.ds(2 * jnp.maximum(block, 0), 1), :]
                keys = jnp.where(block >= 0, keys, -1)
            else:
                over = i + j >= 2 * CHIPS
                keys = seg[pl.ds(jnp.where(over, 2 * (4 * CHIPS - 1 - i - j), 2 * (i + j) + 1), 1), :]
            allowed = asks == keys
            if j == (REACH if b == 0 else 0):
                allowed = allowed & (lane <= row)
            bias[b, :, j * BLOCK:(j + 1) * BLOCK] = jnp.where(allowed, 0.0, FAR)

    def a2():
        gq.a_step(1)

    def b2():
        gq.b_z(2, -2)
        gq.b_ywait(1, -1)
        gq.b_relay(0, 0)

    both(a2, b2)

    def a3():
        gq.a_step(2)
        gq.a_done(0)

    def b3():
        gq.b_z(3, -3)
        gq.b_ywait(2, -2)
        gq.b_relay(1, 0)
        gq.b_relay(0, 1, -1)

    both(a3, b3)

    def a4():
        gq.a_step(3)
        gq.a_done(1, -1)

    def b4():
        gq.b_z(4)
        gq.b_ywait(3, -3)
        gq.b_relay(1, 1, -1)
        gq.b_relay(0, 2, -2)
        gq.b_ywait(4)
        gq.b_done(0)
        gw.b_start_z()
        gw.b_y(0)

    both(a4, b4)
    loads[5].wait()
    acc[...] = jnp.zeros_like(acc)

    def project(first, last):
        @pl.loop(first, last)
        def _(t):
            zr = ((t + 1) // 2) * (2 * (t % 2) - 1)
            zz = (me.z + zr + NZ) % NZ
            ref = qbuf.at[zz, :, :, 1 - c]
            index = (zr + NZ) % NZ
            pltpu.make_async_remote_copy(
                src_ref=ref, dst_ref=ref, send_sem=qs_s.at[index], recv_sem=qs_r.at[index],
                device_id=me.sibling(), device_id_type=MESH).wait_recv()
            part = NY * NX * 2 * SHARD
            weights = qbuf[zz].reshape(part, QKV)
            acc[...] += jnp.dot(hid[:, pl.ds(pl.multiple_of(zz * part, part), part)], weights,
                                preferred_element_type=jnp.float32)

    def a5():
        gq.a_step(4)
        for j in range(4):
            gw.a_stream(j)
        gw.a_y(0)
        gq.a_done(2, -2)

    def b5():
        gq.b_relay(1, 2, -2)
        gq.b_relay(0, 3, -3)
        gq.b_done(1, -1)
        gw.b_z(1, -1, x=False)

    both(a5, b5)
    project(0, 3)

    def a6():
        gq.a_done(3, -3, 4)
        gw.a_step(1)

    def b6():
        gq.b_relay(1, 3, -3)
        gq.b_relay(0, 4)
        gq.b_relay(1, 4)
        gq.b_done(2, -2, 3, -3, 4)

    both(a6, b6)
    project(3, 8)

    for b in range(2):
        rows = slice(b * BLOCK, (b + 1) * BLOCK)
        slot = REACH + c if b == 0 else c
        for h in range(HQ + 1):
            part = acc[rows, h * HD:(h + 1) * HD]
            turned = part * cos_t[b] + pltpu.roll(part, HD // 2, 1) * sin_t[b]
            turned = turned.astype(jnp.bfloat16)
            if h < HQ:
                qrot[b, h] = turned
            else:
                kvw[b, slot, :, 0:HD] = turned
        kvw[b, slot, :, HD:2 * HD] = acc[rows, QW + HD:QKV].astype(jnp.bfloat16)

    def kv_copy(src, dst, sent, got, device):
        return pltpu.make_async_remote_copy(
            src_ref=src, dst_ref=dst, send_sem=sent, recv_sem=got, device_id=device, device_id_type=MESH)

    early_own, late_own = kvw.at[0, REACH + c], kvw.at[1, c]

    def kv_up(m):
        return kv_copy(early_own, kvw.at[0, REACH - 2 * m + c], kv_s.at[0, m], kv_r.at[0, m], me.on(k + m, c))

    def kv_over(m):
        return kv_copy(early_own, kvw.at[1, 2 * m + 1 - c], kv_s.at[0, m], kv_r.at[1, m],
                       me.on(2 * CHIPS - 1 - k - m, 1 - c))

    def kv_down(m):
        return kv_copy(late_own, kvw.at[1, 2 * m + c], kv_s.at[1, m], kv_r.at[1, m], me.on(k - m, c))

    def kv_side(b, m, core):
        ref = kvw.at[0, REACH - 2 * m + core] if b == 0 else kvw.at[1, 2 * m + core]
        return kv_copy(ref, ref, kvs_s.at[b, m], kvs_r.at[b, m], me.sibling())

    for m in range(4, 0, -1):
        pl.when(k + m < CHIPS)(lambda m=m: kv_up(m).start())
        pl.when(k + m >= CHIPS)(lambda m=m: kv_over(m).start())
        pl.when(k >= m)(lambda m=m: kv_down(m).start())
    for b in range(2):
        kv_side(b, 0, c).start()

    def a7():
        gw.a_step(2)
        gw.a_done(0)

    def b7():
        for zr in (0, 1, -1):
            gw.b_x(zr, 0)
        gw.b_ywait(0, 1, -1)
        gw.b_z(2, -2)
        gw.b_ywait(2, -2)
        gw.b_z(3, -3)
        gw.b_ywait(3, -3)

    both(a7, b7)

    for m in range(1, 5):
        def early_in(m=m):
            kv_copy(early_own, kvw.at[0, REACH - 2 * m + c], kv_s.at[0, m], kv_r.at[0, m], me.sibling()).wait_recv()
            kv_side(0, m, c).start()

        pl.when(k >= m)(early_in)
        kv_copy(late_own, kvw.at[1, 2 * m + c], kv_s.at[1, m], kv_r.at[1, m], me.sibling()).wait_recv()
        kv_side(1, m, c).start()

    def a8():
        gw.a_step(3)
        gw.a_done(1, -1)

    def b8():
        gw.b_z(4)
        gw.b_ywait(4)
        gw.b_relay(0, 0, 1, -1, 2, -2)
        gw.b_relay(1, 0, 1, -1, 2, -2)

    both(a8, b8)

    def attend(b):
        window = kvw.at[b, pl.ds(c, REACH + 1)]
        span = (REACH + 1) * BLOCK
        keys = window[:, :, 0:HD].reshape(span, HD)
        values = window[:, :, HD:2 * HD].reshape(span, HD)
        scale = math.log2(math.e) / math.sqrt(HD)
        scores = lax.dot_general(qrot[b].reshape(HQ * BLOCK, HD), keys, (((1,), (1,)), ((), ())),
                                 preferred_element_type=jnp.float32)
        scores = scores.reshape(HQ, BLOCK, span) * scale + bias[b][None]
        scores = scores.reshape(HQ * BLOCK, span)
        peak = jnp.max(scores, axis=1, keepdims=True)
        terms = jnp.exp2(scores - peak)
        total = jnp.sum(terms, axis=1, keepdims=True)
        weights = (terms * (1.0 / total)).astype(jnp.bfloat16)
        result = jnp.dot(weights, values, preferred_element_type=jnp.float32).astype(jnp.bfloat16)
        for h in range(HQ):
            mixed[b * BLOCK:(b + 1) * BLOCK, h * HD:(h + 1) * HD] = result[h * BLOCK:(h + 1) * BLOCK]

    for m in range(0, 5):
        pl.when(k >= m)(lambda m=m: kv_side(0, m, 1 - c).wait_recv())
        kv_side(1, m, 1 - c).wait_recv()
    attend(0)

    def a9():
        gw.a_step(4)
        gw.a_done(2, -2)

    def b9():
        gw.b_relay(0, 3, -3, 4)
        gw.b_relay(1, 3, -3, 4)
        gw.b_done(0, 1, -1, 2, -2)

    both(a9, b9)
    attend(1)

    def a10():
        gw.a_done(3, -3, 4)

    def b10():
        gw.b_done(3, -3, 4)

    both(a10, b10)

    part = NY * NX * BLOCK

    def out_copy(t):
        zr = ((t + 1) // 2) * (2 * (t % 2) - 1)
        zz = (me.z + zr + NZ) % NZ
        columns = pl.ds(pl.multiple_of(zz * part, part), part)
        return pltpu.make_async_copy(outv.at[:, columns], out_hbm.at[:, columns], out_sem.at[t])

    @pl.loop(0, NZ)
    def _(t):
        zr = ((t + 1) // 2) * (2 * (t % 2) - 1)
        zz = (me.z + zr + NZ) % NZ
        index = (zr + NZ) % NZ

        def wait(core):
            ref = wbuf.at[zz, :, :, pl.ds(*W_ROWS[core]), :]
            pltpu.make_async_remote_copy(
                src_ref=ref, dst_ref=ref, send_sem=ws_s.at[index], recv_sem=ws_r.at[index],
                device_id=me.sibling(), device_id_type=MESH).wait_recv()

        both(lambda: wait(1), lambda: wait(0))
        for pair in range(NY * NX // 2):
            y, x = pair // 2, (pair % 2) * 2
            weights = jnp.concatenate([wbuf[zz, y, x], wbuf[zz, y, x + 1]], axis=1)
            result = jnp.dot(mixed[...], weights, preferred_element_type=jnp.float32)
            start = pl.multiple_of(zz * part + pair * 2 * BLOCK, 2 * BLOCK)
            outv[:, pl.ds(start, 2 * BLOCK)] = result.astype(jnp.bfloat16)
        out_copy(t).start()

    def finish(core):
        gq.drain(core)
        gw.drain(core)

    both(lambda: finish(0), lambda: finish(1))
    for m in range(1, 5):
        kv_copy(early_own, early_own, kv_s.at[0, m], kv_r.at[0, m], me.sibling()).wait_send()
        pl.when(k >= m)(lambda m=m: kv_down(m).wait_send())
    for m in range(0, 5):
        pl.when(k >= m)(lambda m=m: kv_side(0, m, c).wait_send())
        kv_side(1, m, c).wait_send()

    @pl.loop(0, NZ)
    def _(t):
        out_copy(t).wait()


def on_device(hidden_in, segment_ids, w_query, w_key, w_value, w_out):
    half = np.arange(HD // 2, dtype=np.float32) * np.float32(2.0) / np.float32(HD)
    freq = np.power(np.float32(ROPE_BASE), -half).astype(np.float32)
    freq = jnp.asarray(np.concatenate([freq, freq])[None, :])
    seg = segment_ids.reshape(4 * CHIPS, BLOCK)
    rows = hidden_in.shape[0]
    anywhere = pl.BlockSpec(memory_space=pl.ANY)
    dma = pltpu.SemaphoreType.DMA
    bf16, f32 = jnp.bfloat16, jnp.float32
    return pl.pallas_call(
        kernel,
        out_shape=jax.ShapeDtypeStruct((rows, D), bf16),
        in_specs=[anywhere] * 6 + [pl.BlockSpec(memory_space=pltpu.VMEM)],
        out_specs=anywhere,
        scratch_shapes=[
            pltpu.VMEM((rows, D), bf16),
            pltpu.VMEM((4 * CHIPS, BLOCK), jnp.int32),
            pltpu.VMEM((NZ, NY, NX, 2, SHARD, QKV), bf16),
            pltpu.VMEM((NZ, NY, NX, QW, BLOCK), bf16),
            pltpu.VMEM((QW, SHARD), bf16),
            pltpu.VMEM((QW, SHARD), bf16),
            pltpu.VMEM((rows, QKV), f32),
            pltpu.VMEM((2, BLOCK, HD), f32),
            pltpu.VMEM((2, BLOCK, HD), f32),
            pltpu.VMEM((2, BLOCK, (REACH + 1) * BLOCK), f32),
            pltpu.VMEM((2, HQ, BLOCK, HD), bf16),
            pltpu.VMEM((2, REACH + 2, BLOCK, 2 * HD), bf16),
            pltpu.VMEM((rows, QW), bf16),
            pltpu.VMEM((rows, D), bf16),
            dma((6,)), dma((NZ,)), dma, dma,
            dma((112,)), dma((112,)), dma((NZ,)), dma((NZ,)),
            dma((112,)), dma((112,)), dma((NZ,)), dma((NZ,)),
            dma((2, 5)), dma((2, 5)), dma((2, 5)), dma((2, 5)),
        ],
        compiler_params=pltpu.CompilerParams(
            collective_id=1, has_side_effects=True, vmem_limit_bytes=60 * 2**20),
        name="layer",
    )(hidden_in, seg, w_query, w_key, w_value, w_out, freq)


def solution(mesh):
    in_specs = (
        P(("dp", "ctx"), None),
        P("dp"),
        P("ctx", None),
        P("ctx", None),
        P("ctx", None),
        P(None, "ctx"),
    )
    out_specs = P(("dp", "ctx"), None)
    return jax.shard_map(
        on_device, mesh=mesh, in_specs=in_specs, out_specs=out_specs, check_vma=False
    )
```

time: 898 us -> 86.4 us (0.10)
  the two profiles are of different devices: /device:TPU:9 before, /device:TPU:1 now
where the time goes in v1:
time: 86.4 us; the launch traced here: 86.2 us
  Pallas kernels  80 us (93%)
  local copies, waits for them, and re-layouts  6.24 us (7%)
    pallas_call x1, Pallas kernels, on_device(): pl.pallas_call(kernel, out_shape=jax.ShapeDtypeStruct((rows, D), bf16), i...  80 us
    unnamed x2, local copies, waits for them, and re-layouts  6.24 us

profile of v1, /device:TPU:1, one launch (start us, length us, event | category | flops | bytes accessed | tf_op | source)
XLA Modules:
  0.0 86.2 jit_solution(3843538764993747768)
XLA Ops:
  0.0 1.6 %copy.8.wo_hbm = bf16[512,64]{1,0:T(8,128)(2,1)} copy(bf16[512,64]{0,1:T(8,128)(2,1)} %param.12) | data formatting | bytes 131072 | tf_op args[5]
  1.6 80.0 %layer.1 = bf16[256,8192]{1,0:T(8,128)(2,1)} custom-call(bf16[256,8192]{1,0:T(8,128)(2,1)} %hid_hbm.1, s32[256,128]{1,0:T(8,128)} %bitcast.1, bf16[64,512]{1,0:T(8,128)(2,1)} %wq_hbm.1, bf16[64,128]{1,0:T(8,128)(2,1)} %wk_hbm.1, bf16[64,128]{1,0:T(8,128)(2,1)} %wv_hbm.1, bf16[512,64]{1,0:T(8,128)(2,1)} %copy.8.wo_hbm, f32[1,128]{1,0:T(1,128)} %constant.2.clone.freq_ref), custom_call_target="tpu_custom_call" | custom-call | tf_op jit(solution)/shard_map/layer/pallas_call | solution.py:581
  81.6 4.6 %copy.10 = bf16[256,8192]{1,0:T(8,128)(2,1)} copy(bf16[256,8192]{1,0:T(8,128)(2,1)} %layer.1) | data formatting | bytes 8388608

commit v2 on v1

v2 whole, which is shorter than its diff:
```python
import functools
import math

import jax
import jax.numpy as jnp
import numpy as np
from jax import lax
from jax.experimental import pallas as pl
from jax.experimental.pallas import tpu as pltpu
from jax.sharding import PartitionSpec as P

MESH = pl.DeviceIdType.MESH
REACH = 8
ROPE_BASE = 500000.0
NZ, NY, NX = 8, 2, 4
CHIPS = NZ * NY * NX
BLOCK = 128
HD = 128
HQ = 4
D = 8192
QW = HQ * HD
QKV = QW + 2 * HD
SHARD = 64
ORDER = (0, 1, -1, 2, -2, 3, -3, 4)
FAR = -1e30
W_ROWS = ((0, 384), (384, 128))


SIDE = (0, -1, 1, 2)
DIRECT = (2, 1)
PLAN = (
    (
        (("q","x",1),("q","x",2),("q","z",0,1,1),("q","z",0,-1,1),("q","x",3),("q","y",0),("q","z",1,1,1),("q","z",1,-1,1),("q","z",2,1,1),("q","z",2,-1,1),("q","z",0,1,2),("q","z",0,-1,2),("q","z",3,1,1),("q","z",3,-1,1),("q","y",1),("q","y",-1),("q","d",0),("w","s"),("q","z",1,1,2),("q","z",1,-1,2),("q","z",2,1,2),("q","z",2,-1,2),("q","z",0,1,3),("q","z",0,-1,3),("q","d",1),("q","z",3,1,2),("q","z",3,-1,2),("q","y",2),("q","y",-2),("w","x",2),),
        (("w","x",1),("w","z",0,1,1),("w","z",0,-1,1),("q","d",-1),("q","z",1,1,3),("q","z",1,-1,3),("q","z",2,1,3),("q","z",2,-1,3),("q","f",0),("q","d",2),("q","z",3,1,3),("q","z",3,-1,3),("q","y",3),("q","y",-3),("w","z",2,1,1),("w","z",2,-1,1),("q","d",-2),("w","z",1,1,1),("w","z",1,-1,1),("w","x",3),("w","y",0),("w","z",0,1,2),("w","z",0,-1,2),),
        (("q","f",1),("q","f",2),("q","d",3),("q","f",3),("q","y",4),("w","z",2,1,2),("w","z",2,-1,2),("q","d",-3),("w","z",1,1,2),("w","z",1,-1,2),("w","z",3,1,1),("w","z",3,-1,1),("w","y",1),("w","y",-1),("w","d",0),("w","z",0,1,3),("w","z",0,-1,3),("w","z",2,1,3),("w","z",2,-1,3),),
        (("q","d",4),("w","z",1,1,3),("w","z",1,-1,3),("w","z",3,1,2),("w","z",3,-1,2),("w","y",2),("w","y",-2),("w","f",0),("w","d",1),("w","f",2),("w","f",1),("w","d",-1),("w","z",3,1,3),("w","z",3,-1,3),("w","y",3),("w","y",-3),),
        (("w","d",2),("w","f",3),("w","y",4),),
        (("w","d",-2),("w","d",3),("w","d",-3),("w","d",4),),
        (),
        (),
        (),
        (),
        (),
        (),
    ),
    (
        (("q","y",0),("q","z",-1),("q","z",1),("q","y",-1),("q","z",2),("q","z",-2),("q","y",1),("q","r",0,-1),("q","r",0,1),("q","r",-1,-1),("q","r",-1,1),("q","y",2),("q","z",3),("q","z",-3),("q","y",-2),("w","s"),("q","r",1,-1),("q","r",1,1),("q","d",0),),
        (("q","d",-1),("q","r",2,-1),("q","z",4),("w","z",-1),("q","y",3),("w","z",1),("q","y",-3),("w","y",0),("q","r",2,1),("q","r",-2,-1),("q","r",-2,1),("q","y",4),("q","d",1),("w","y",-1),("w","y",1),),
        (("w","z",2),("w","z",-2),("q","r",3,-1),("q","r",-3,-1),("q","r",3,1),("w","r",0,-1),("q","r",-3,1),("w","r",0,1),("q","r",4,-1),("w","r",-1,-1),("q","d",2),("w","r",1,-1),("w","y",2),("w","y",-2),("q","d",-2),),
        (("w","z",3),("w","z",-3),("q","r",4,1),("w","r",1,1),("w","r",-1,1),("q","d",3),("w","r",2,-1),("q","d",-3),("w","z",4),("w","d",0),("w","r",-2,-1),("w","r",2,1),("w","r",-2,1),("w","y",3),("w","y",-3),("q","d",4),),
        (("w","d",1),("w","d",-1),("w","d",2),("w","r",3,-1),("w","d",-2),("w","r",3,1),("w","r",-3,-1),("w","r",-3,1),),
        (("w","y",4),("w","d",3),("w","d",-3),("w","r",4,1),("w","r",4,-1),),
        (("w","d",4),),
        (),
        (),
        (),
        (),
        (),
    ),
)


class Gather:
    def __init__(self, direct, place, ssem, rsem, sib_r, slot, most):
        self.direct, self.place = direct, place
        self.ssem, self.rsem, self.sib_r = ssem, rsem, sib_r
        self.slot, self.most = slot, most
        self.keys = ({}, {})

    def copy(self, ref, sem, device):
        return pltpu.make_async_remote_copy(
            src_ref=ref, dst_ref=ref, send_sem=self.ssem, recv_sem=sem, device_id=device, device_id_type=MESH)

    def sem(self, core, key):
        table = self.keys[core]
        return self.rsem.at[table.setdefault(key, len(table))]

    def send(self, core, where, key, move):
        self.copy(self.slot(core, *where), self.sem(core, key), self.place.at(*move)).start()

    def recv(self, core, where, key):
        self.copy(self.slot(core, *where), self.sem(core, key), self.place.sibling()).wait_recv()

    def sib(self, core, zr, part):
        where = (zr, part, None, None) if core == 0 else (zr, None, part, None)
        self.copy(self.slot(core, *where), self.sib_r.at[(zr + NZ) % NZ], self.place.sibling()).start()

    def sib_recv(self, core, zr):
        index = (zr + NZ) % NZ
        self.copy(self.slot(core, zr, None, None, None), self.sib_r.at[index], self.place.sibling()).wait_recv()

    def drain(self, core):
        for ref in self.most(core):
            self.copy(ref, self.sib_r.at[0], self.place.sibling()).wait_send()

    def a_s(self):
        for step in (1, -1, 2):
            self.send(0, (0, 0, 0, None), ("X", step), (0, 0, step))
        self.a_up(0)

    def a_up(self, j):
        for way in (1, -1):
            self.send(0, (0, 0, SIDE[j], None), ("Z", j, way, 1), (way, 0, 0))

    def a_x(self, j):
        self.recv(0, (0, 0, SIDE[j], None), ("X", -SIDE[j] if j < 3 else 2))
        self.a_up(j)

    def a_z(self, j, way, s):
        self.recv(0, (-way * s, 0, SIDE[j], None), ("Z", j, way, s))
        if s < 3:
            self.send(0, (-way * s, 0, SIDE[j], None), ("Z", j, way, s + 1), (way, 0, 0))
        else:
            self.send(0, (-way * s, 0, SIDE[j], (1 - way) // 2), ("Z", j), (way, 0, 0))

    def a_f(self, j):
        self.recv(0, (4, 0, SIDE[j], None), ("Z", j))

    def a_y(self, zr):
        for way in (1, -1):
            self.send(0, (zr, 0, None, (1 - way) // 2), ("Y", zr), (0, way, 0))
        self.sib(0, zr, 0)

    def a_d(self, zr):
        self.recv(0, (zr, 1, None, None), ("Y", zr))
        self.sib(0, zr, 1)

    def b_s(self):
        self.b_fan(0, 0)
        for far in range(1, self.direct + 1):
            for way in (1, -1):
                self.send(1, (0, 0, 0, None), ("Z", way, far), (way * far, 0, 0))
        self.b_cross(0)

    def b_fan(self, zr, yr):
        for way in (1, -1):
            self.send(1, (zr, yr, 0, None), ("X", zr, way), (0, 0, way))

    def b_cross(self, zr):
        for way in (1, -1):
            self.send(1, (zr, 0, 0, (1 - way) // 2), ("Y", zr), (0, way, 0))

    def b_z(self, zr):
        if zr == 4:
            self.recv(1, (4, 0, 0, None), ("Z", 4))
        else:
            way, far = (-1 if zr > 0 else 1), abs(zr)
            self.recv(1, (zr, 0, 0, None), ("Z", way, far))
            if far == 3:
                self.send(1, (zr, 0, 0, (1 - way) // 2), ("Z", 4), (way, 0, 0))
            elif far + 1 > self.direct:
                self.send(1, (zr, 0, 0, None), ("Z", way, far + 1), (way, 0, 0))
        self.b_fan(zr, 0)
        self.b_cross(zr)

    def b_y(self, zr):
        self.recv(1, (zr, 1, 0, None), ("Y", zr))
        self.b_fan(zr, 1)
        self.sib(1, zr, 0)

    def b_r(self, zr, way):
        self.recv(1, (zr, None, -way, None), ("X", zr, way))
        self.send(1, (zr, None, -way, (1 - way) // 2), ("XR", zr), (0, 0, way))
        self.sib(1, zr, -way)

    def b_d(self, zr):
        self.recv(1, (zr, None, 2, None), ("XR", zr))
        self.sib(1, zr, 2)


class Place:
    def __init__(self):
        ctx, dp = lax.axis_index("ctx"), lax.axis_index("dp")
        self.ctx, self.dp = ctx, dp
        self.c = ctx % 2
        self.k = ctx // 2
        self.x = self.k % NX
        self.yl = (self.k // NX) % NY
        self.z = self.k // (NX * NY)
        self.y = dp * 2 + self.yl

    def zi(self, zr):
        return (self.z + (zr + NZ)) % NZ

    def yi(self, yr):
        return (self.yl + yr) % NY

    def xi(self, xr):
        return (self.x + (xr + NX)) % NX

    def at(self, dz, dy, dx):
        y = (self.y + (dy + 4)) % 4
        chip = (self.zi(dz) * NY + y % 2) * NX + self.xi(dx)
        return {"ctx": chip * 2 + self.c, "dp": y // 2}

    def sibling(self):
        return {"ctx": self.k * 2 + (1 - self.c), "dp": self.dp}

    def on(self, chip, core):
        return {"ctx": chip * 2 + core, "dp": self.dp}


def kernel(hid_hbm, seg_hbm, wq_hbm, wk_hbm, wv_hbm, wo_hbm, freq_ref, out_hbm,
           hid, seg, qbuf, wbuf, wo_in, wo_sib, acc, cos_t, sin_t, bias, qrot, kvw, mixed, outv,
           load_sem, out_sem, wo_s, wo_r, q_s, q_r, qs_r, w_s, w_r, ws_r,
           kv_s, kv_r, kvs_s, kvs_r):
    me = Place()
    c, k, i = me.c, me.k, me.ctx

    def chips(zr, yr, xr):
        every = slice(None)
        return me.zi(zr), every if yr is None else me.yi(yr), every if xr is None else me.xi(xr)

    def q_slot(core, zr, yr, xr, half):
        rows = pl.ds(0, SHARD) if half is None else pl.ds(half * (SHARD // 2), SHARD // 2)
        return qbuf.at[*chips(zr, yr, xr), core, rows, :]

    def q_most(core):
        return (qbuf.at[:, :, :, core], qbuf.at[0:NZ - 1, :, :, core],
                qbuf.at[NZ - 1, 0, :, core], qbuf.at[NZ - 1, 1, 0:NX - 1, core])

    def w_slot(core, zr, yr, xr, half):
        first, count = W_ROWS[core]
        rows = pl.ds(first, count) if half is None else pl.ds(first + half * (count // 2), count // 2)
        return wbuf.at[*chips(zr, yr, xr), rows, :]

    def w_most(core):
        rows = pl.ds(*W_ROWS[core])
        return (wbuf.at[:, :, :, rows], wbuf.at[0:NZ - 1, :, :, rows],
                wbuf.at[NZ - 1, 0, :, rows], wbuf.at[NZ - 1, 1, 0:NX - 1, rows])

    gq = Gather(DIRECT[0], me, q_s, q_r, qs_r, q_slot, q_most)
    gw = Gather(DIRECT[1], me, w_s, w_r, ws_r, w_slot, w_most)

    def both(first, second):
        pl.when(c == 0)(first)
        pl.when(c == 1)(second)

    own = qbuf.at[me.z, me.yl, me.x, c]
    loads = [
        pltpu.make_async_copy(wq_hbm, own.at[:, pl.ds(0, QW)], load_sem.at[0]),
        pltpu.make_async_copy(wk_hbm, own.at[:, pl.ds(QW, HD)], load_sem.at[1]),
        pltpu.make_async_copy(wv_hbm, own.at[:, pl.ds(QW + HD, HD)], load_sem.at[2]),
        pltpu.make_async_copy(wo_hbm, wo_in, load_sem.at[3]),
        pltpu.make_async_copy(seg_hbm, seg, load_sem.at[4]),
        pltpu.make_async_copy(hid_hbm, hid, load_sem.at[5]),
    ]
    for load in loads:
        load.start()

    kvw[0, 0:REACH] = jnp.zeros((REACH, BLOCK, 2 * HD), jnp.bfloat16)

    def up(m):
        over = k + m >= CHIPS
        return (jnp.where(over, 2 * CHIPS - 1 - k - m, k + m), jnp.where(over, 1 - c, c))

    barrier = pltpu.get_barrier_semaphore()

    def greet(device):
        pl.semaphore_signal(barrier, inc=1, device_id=device, device_id_type=MESH)

    moves = [(0, 0, 1), (0, 0, -1), (0, 0, 2), (0, 1, 0), (0, -1, 0)]
    moves += [(way * far, 0, 0) for far in (1, 2, 3) for way in (1, -1)]
    for move in moves:
        greet(me.at(*move))
    greet(me.sibling())
    for m in range(1, 5):
        greet(me.on(*up(m)))
        pl.when(k >= m)(lambda m=m: greet(me.on(k - m, c)))
    pl.semaphore_wait(barrier, len(moves) + 5 + jnp.minimum(k, 4))

    for load in loads[:3]:
        load.wait()

    gathers = {"q": gq, "w": gw}

    def run(step):
        def core(which):
            for op in PLAN[which][step]:
                if op[:2] == ("w", "s"):
                    join(which)
                getattr(gathers[op[0]], "ab"[which] + "_" + op[1])(*op[2:])

        both(lambda: core(0), lambda: core(1))

    wo_copy = pltpu.make_async_remote_copy(
        src_ref=wo_in, dst_ref=wo_sib, send_sem=wo_s, recv_sem=wo_r,
        device_id=me.sibling(), device_id_type=MESH)

    def join(core):
        wo_copy.wait()
        rows = pl.ds(*W_ROWS[core])
        pair = [wo_in[:, rows], wo_sib[:, rows]]
        block = jnp.concatenate(pair if core == 0 else pair[::-1], axis=0)
        wbuf[me.z, me.yl, me.x, rows, :] = jnp.transpose(block)

    both(gq.a_s, gq.b_s)
    loads[3].wait()
    wo_copy.start()
    row = lax.broadcasted_iota(jnp.int32, (BLOCK, HD), 0)
    lane = lax.broadcasted_iota(jnp.int32, (BLOCK, HD), 1)
    late = 2 * 2 * CHIPS - 1 - i
    for b, block in enumerate((i, late)):
        angle = (block * BLOCK + row).astype(jnp.float32) * freq_ref[...]
        cos_t[b] = jnp.cos(angle)
        sine = jnp.sin(angle)
        sin_t[b] = jnp.where(lane < HD // 2, -sine, sine)

    loads[4].wait()
    for b in range(2):
        mine = seg[pl.ds(2 * i + b, 1), :]
        asks = jnp.transpose(jnp.broadcast_to(mine, (BLOCK, BLOCK)))
        for j in range(REACH + 1):
            if b == 0:
                block = i - REACH + j
                keys = seg[pl.ds(2 * jnp.maximum(block, 0), 1), :]
                keys = jnp.where(block >= 0, keys, -1)
            else:
                over = i + j >= 2 * CHIPS
                keys = seg[pl.ds(jnp.where(over, 2 * (4 * CHIPS - 1 - i - j), 2 * (i + j) + 1), 1), :]
            allowed = asks == keys
            if j == (REACH if b == 0 else 0):
                allowed = allowed & (lane <= row)
            bias[b, :, j * BLOCK:(j + 1) * BLOCK] = jnp.where(allowed, 0.0, FAR)

    loads[5].wait()
    acc[...] = jnp.zeros_like(acc)

    def project(first, last):
        @pl.loop(first, last)
        def _(t):
            zr = ((t + 1) // 2) * (2 * (t % 2) - 1)
            zz = (me.z + zr + NZ) % NZ
            both(lambda: gq.sib_recv(1, zr), lambda: gq.sib_recv(0, zr))
            part = NY * NX * 2 * SHARD
            weights = qbuf[zz].reshape(part, QKV)
            acc[...] += jnp.dot(hid[:, pl.ds(pl.multiple_of(zz * part, part), part)], weights,
                                preferred_element_type=jnp.float32)

    edges = (0, 1, 3, 5, 8)
    for n in range(4):
        run(n)
        project(edges[n], edges[n + 1])
    run(4)

    for b in range(2):
        rows = slice(b * BLOCK, (b + 1) * BLOCK)
        slot = REACH + c if b == 0 else c
        for h in range(HQ + 1):
            part = acc[rows, h * HD:(h + 1) * HD]
            turned = part * cos_t[b] + pltpu.roll(part, HD // 2, 1) * sin_t[b]
            turned = turned.astype(jnp.bfloat16)
            if h < HQ:
                qrot[b, h] = turned
            else:
                kvw[b, slot, :, 0:HD] = turned
        kvw[b, slot, :, HD:2 * HD] = acc[rows, QW + HD:QKV].astype(jnp.bfloat16)

    def kv_copy(src, dst, sent, got, device):
        return pltpu.make_async_remote_copy(
            src_ref=src, dst_ref=dst, send_sem=sent, recv_sem=got, device_id=device, device_id_type=MESH)

    early_own, late_own = kvw.at[0, REACH + c], kvw.at[1, c]

    def kv_up(m):
        return kv_copy(early_own, kvw.at[0, REACH - 2 * m + c], kv_s.at[0, m], kv_r.at[0, m], me.on(k + m, c))

    def kv_over(m):
        return kv_copy(early_own, kvw.at[1, 2 * m + 1 - c], kv_s.at[0, m], kv_r.at[1, m],
                       me.on(2 * CHIPS - 1 - k - m, 1 - c))

    def kv_down(m):
        return kv_copy(late_own, kvw.at[1, 2 * m + c], kv_s.at[1, m], kv_r.at[1, m], me.on(k - m, c))

    def kv_side(b, m, core):
        ref = kvw.at[0, REACH - 2 * m + core] if b == 0 else kvw.at[1, 2 * m + core]
        return kv_copy(ref, ref, kvs_s.at[b, m], kvs_r.at[b, m], me.sibling())

    for m in range(4, 0, -1):
        pl.when(k + m < CHIPS)(lambda m=m: kv_up(m).start())
        pl.when(k + m >= CHIPS)(lambda m=m: kv_over(m).start())
        pl.when(k >= m)(lambda m=m: kv_down(m).start())
    for b in range(2):
        kv_side(b, 0, c).start()

    run(5)
    for m in range(1, 5):
        def early_in(m=m):
            kv_copy(early_own, kvw.at[0, REACH - 2 * m + c], kv_s.at[0, m], kv_r.at[0, m], me.sibling()).wait_recv()
            kv_side(0, m, c).start()

        pl.when(k >= m)(early_in)
        kv_copy(late_own, kvw.at[1, 2 * m + c], kv_s.at[1, m], kv_r.at[1, m], me.sibling()).wait_recv()
        kv_side(1, m, c).start()

    run(6)

    def attend(b):
        window = kvw.at[b, pl.ds(c, REACH + 1)]
        span = (REACH + 1) * BLOCK
        keys = window[:, :, 0:HD].reshape(span, HD)
        values = window[:, :, HD:2 * HD].reshape(span, HD)
        scale = math.log2(math.e) / math.sqrt(HD)
        scores = lax.dot_general(qrot[b].reshape(HQ * BLOCK, HD), keys, (((1,), (1,)), ((), ())),
                                 preferred_element_type=jnp.float32)
        scores = scores.reshape(HQ, BLOCK, span) * scale + bias[b][None]
        scores = scores.reshape(HQ * BLOCK, span)
        peak = jnp.max(scores, axis=1, keepdims=True)
        terms = jnp.exp2(scores - peak)
        total = jnp.sum(terms, axis=1, keepdims=True)
        weights = (terms * (1.0 / total)).astype(jnp.bfloat16)
        result = jnp.dot(weights, values, preferred_element_type=jnp.float32).astype(jnp.bfloat16)
        for h in range(HQ):
            mixed[b * BLOCK:(b + 1) * BLOCK, h * HD:(h + 1) * HD] = result[h * BLOCK:(h + 1) * BLOCK]

    for m in range(0, 5):
        pl.when(k >= m)(lambda m=m: kv_side(0, m, 1 - c).wait_recv())
        kv_side(1, m, 1 - c).wait_recv()
    attend(0)

    run(7)
    attend(1)

    part = NY * NX * BLOCK

    def out_copy(t):
        zr = ((t + 1) // 2) * (2 * (t % 2) - 1)
        zz = (me.z + zr + NZ) % NZ
        columns = pl.ds(pl.multiple_of(zz * part, part), part)
        return pltpu.make_async_copy(outv.at[:, columns], out_hbm.at[:, columns], out_sem.at[t])

    def emit(t):
        zr = ((t + 1) // 2) * (2 * (t % 2) - 1)
        zz = (me.z + zr + NZ) % NZ
        both(lambda: gw.sib_recv(1, zr), lambda: gw.sib_recv(0, zr))
        for pair in range(NY * NX // 2):
            y, x = pair // 2, (pair % 2) * 2
            weights = jnp.concatenate([wbuf[zz, y, x], wbuf[zz, y, x + 1]], axis=1)
            result = jnp.dot(mixed[...], weights, preferred_element_type=jnp.float32)
            start = pl.multiple_of(zz * part + pair * 2 * BLOCK, 2 * BLOCK)
            outv[:, pl.ds(start, 2 * BLOCK)] = result.astype(jnp.bfloat16)
        out_copy(t).start()

    for n in range(3):
        run(8 + n)
        pl.loop(edges[n + 1] if n else 0, edges[n + 2])(emit)

    def finish(core):
        gq.drain(core)
        gw.drain(core)

    both(lambda: finish(0), lambda: finish(1))
    for m in range(1, 5):
        kv_copy(early_own, early_own, kv_s.at[0, m], kv_r.at[0, m], me.sibling()).wait_send()
        pl.when(k >= m)(lambda m=m: kv_down(m).wait_send())
    for m in range(0, 5):
        pl.when(k >= m)(lambda m=m: kv_side(0, m, c).wait_send())
        kv_side(1, m, c).wait_send()

    @pl.loop(0, NZ)
    def _(t):
        out_copy(t).wait()


def on_device(hidden_in, segment_ids, w_query, w_key, w_value, w_out):
    half = np.arange(HD // 2, dtype=np.float32) * np.float32(2.0) / np.float32(HD)
    freq = np.power(np.float32(ROPE_BASE), -half).astype(np.float32)
    freq = jnp.asarray(np.concatenate([freq, freq])[None, :])
    seg = segment_ids.reshape(4 * CHIPS, BLOCK)
    rows = hidden_in.shape[0]
    anywhere = pl.BlockSpec(memory_space=pl.ANY)
    dma = pltpu.SemaphoreType.DMA
    bf16, f32 = jnp.bfloat16, jnp.float32
    return pl.pallas_call(
        kernel,
        out_shape=jax.ShapeDtypeStruct((rows, D), bf16),
        in_specs=[anywhere] * 6 + [pl.BlockSpec(memory_space=pltpu.VMEM)],
        out_specs=anywhere,
        scratch_shapes=[
            pltpu.VMEM((rows, D), bf16),
            pltpu.VMEM((4 * CHIPS, BLOCK), jnp.int32),
            pltpu.VMEM((NZ, NY, NX, 2, SHARD, QKV), bf16),
            pltpu.VMEM((NZ, NY, NX, QW, BLOCK), bf16),
            pltpu.VMEM((SHARD, QW), bf16),
            pltpu.VMEM((SHARD, QW), bf16),
            pltpu.VMEM((rows, QKV), f32),
            pltpu.VMEM((2, BLOCK, HD), f32),
            pltpu.VMEM((2, BLOCK, HD), f32),
            pltpu.VMEM((2, BLOCK, (REACH + 1) * BLOCK), f32),
            pltpu.VMEM((2, HQ, BLOCK, HD), bf16),
            pltpu.VMEM((2, REACH + 2, BLOCK, 2 * HD), bf16),
            pltpu.VMEM((rows, QW), bf16),
            pltpu.VMEM((rows, D), bf16),
            dma((6,)), dma((NZ,)), dma, dma,
            dma, dma((40,)), dma((NZ,)),
            dma, dma((40,)), dma((NZ,)),
            dma((2, 5)), dma((2, 5)), dma((2, 5)), dma((2, 5)),
        ],
        compiler_params=pltpu.CompilerParams(
            collective_id=1, has_side_effects=True, vmem_limit_bytes=60 * 2**20),
        name="layer",
    )(hidden_in, seg, w_query, w_key, w_value, w_out.T, freq)


def solution(mesh):
    in_specs = (
        P(("dp", "ctx"), None),
        P("dp"),
        P("ctx", None),
        P("ctx", None),
        P("ctx", None),
        P(None, "ctx"),
    )
    out_specs = P(("dp", "ctx"), None)
    return jax.shard_map(
        on_device, mesh=mesh, in_specs=in_specs, out_specs=out_specs, check_vma=False
    )
```

time: 86.4 us -> 82.2 us (0.951)
  the two profiles are of different devices: /device:TPU:1 before, /device:TPU:9 now
where the time goes in v2:
time: 82.2 us; the launch traced here: 82.1 us
  Pallas kernels  77.4 us (94%)
  local copies, waits for them, and re-layouts  4.64 us (6%)
    pallas_call x1, Pallas kernels, on_device(): pl.pallas_call(kernel, out_shape=jax.ShapeDtypeStruct((rows, D), bf16), i...  77.4 us
    unnamed x1, local copies, waits for them, and re-layouts  4.64 us

profile of v2, /device:TPU:9, one launch (start us, length us, event | category | flops | bytes accessed | tf_op | source)
XLA Modules:
  0.0 82.1 jit_solution(15175950395504434393)
XLA Ops:
  0.0 77.4 %layer.1 = bf16[256,8192]{1,0:T(8,128)(2,1)} custom-call(bf16[256,8192]{1,0:T(8,128)(2,1)} %hid_hbm.1, s32[256,128]{1,0:T(8,128)} %bitcast.2, bf16[64,512]{1,0:T(8,128)(2,1)} %wq_hbm.1, bf16[64,128]{1,0:T(8,128)(2,1)} %wk_hbm.1, bf16[64,128]{1,0:T(8,128)(2,1)} %wv_hbm.1, bf16[64,512]{1,0:T(8,128)(2,1)} %bitcast.3, f32[1,128]{1,0:T(1,128)} %constant.2.clone.freq_ref), custom_call_target="tpu_custom_call" | custom-call | tf_op jit(solution)/shard_map/layer/pallas_call | solution.py:474
  77.4 4.6 %copy.9 = bf16[256,8192]{1,0:T(8,128)(2,1)} copy(bf16[256,8192]{1,0:T(8,128)(2,1)} %layer.1) | data formatting | bytes 8388608

commit v3 on v2

--- a/solution.py
+++ b/solution.py
@@ -27,32 +27,43 @@
 
 
 SIDE = (0, -1, 1, 2)
-DIRECT = (2, 1)
+DIRECT = (1, 2, 1)
+RELAY = (False, False, True)
 PLAN = (
     (
-        (("q","x",1),("q","x",2),("q","z",0,1,1),("q","z",0,-1,1),("q","x",3),("q","y",0),("q","z",1,1,1),("q","z",1,-1,1),("q","z",2,1,1),("q","z",2,-1,1),("q","z",0,1,2),("q","z",0,-1,2),("q","z",3,1,1),("q","z",3,-1,1),("q","y",1),("q","y",-1),("q","d",0),("w","s"),("q","z",1,1,2),("q","z",1,-1,2),("q","z",2,1,2),("q","z",2,-1,2),("q","z",0,1,3),("q","z",0,-1,3),("q","d",1),("q","z",3,1,2),("q","z",3,-1,2),("q","y",2),("q","y",-2),("w","x",2),),
-        (("w","x",1),("w","z",0,1,1),("w","z",0,-1,1),("q","d",-1),("q","z",1,1,3),("q","z",1,-1,3),("q","z",2,1,3),("q","z",2,-1,3),("q","f",0),("q","d",2),("q","z",3,1,3),("q","z",3,-1,3),("q","y",3),("q","y",-3),("w","z",2,1,1),("w","z",2,-1,1),("q","d",-2),("w","z",1,1,1),("w","z",1,-1,1),("w","x",3),("w","y",0),("w","z",0,1,2),("w","z",0,-1,2),),
-        (("q","f",1),("q","f",2),("q","d",3),("q","f",3),("q","y",4),("w","z",2,1,2),("w","z",2,-1,2),("q","d",-3),("w","z",1,1,2),("w","z",1,-1,2),("w","z",3,1,1),("w","z",3,-1,1),("w","y",1),("w","y",-1),("w","d",0),("w","z",0,1,3),("w","z",0,-1,3),("w","z",2,1,3),("w","z",2,-1,3),),
-        (("q","d",4),("w","z",1,1,3),("w","z",1,-1,3),("w","z",3,1,2),("w","z",3,-1,2),("w","y",2),("w","y",-2),("w","f",0),("w","d",1),("w","f",2),("w","f",1),("w","d",-1),("w","z",3,1,3),("w","z",3,-1,3),("w","y",3),("w","y",-3),),
-        (("w","d",2),("w","f",3),("w","y",4),),
-        (("w","d",-2),("w","d",3),("w","d",-3),("w","d",4),),
-        (),
-        (),
-        (),
-        (),
-        (),
+        (("k","s"),("q","s"),),
+        (("k","x",1),("k","x",2),("k","z",0,1,1),("k","z",0,-1,1),("q","z",0,1,1),("q","z",0,-1,1),("q","x",1),("q","x",2),("k","x",3),("k","y",0),("k","z",1,1,1),("k","z",1,-1,1),("k","z",2,1,1),("k","z",2,-1,1),("k","z",0,1,2),("k","z",0,-1,2),("q","x",3),("q","y",0),("q","z",0,1,2),("q","z",0,-1,2),("k","d",0),("q","z",1,1,1),("q","z",1,-1,1),("k","z",3,1,1),("k","z",3,-1,1),("k","y",1),("k","y",-1),("k","z",1,1,2),("k","z",1,-1,2),("k","z",2,1,2),("k","z",2,-1,2),("k","z",0,1,3),("k","z",0,-1,3),("q","z",2,1,1),("q","z",2,-1,1),("q","d",0),("q","z",3,1,1),("q","z",3,-1,1),("q","y",1),),
+        (("q","z",0,1,3),("q","y",-1),("q","z",0,-1,3),("k","d",1),("q","z",1,1,2),("q","z",1,-1,2),("k","z",3,1,2),("k","z",3,-1,2),("k","y",2),("k","y",-2),("k","d",-1),("k","z",1,1,3),("k","z",1,-1,3),("k","z",2,1,3),("k","z",2,-1,3),),
+        (("k","f",0),("q","z",2,1,2),("q","z",2,-1,2),("q","z",3,1,2),("q","z",3,-1,2),("q","y",2),("q","y",-2),("q","d",1),("q","f",0),("q","z",1,1,3),("q","z",1,-1,3),("k","z",3,1,3),("k","z",3,-1,3),("k","y",3),("k","y",-3),("k","f",1),("k","f",2),("q","d",-1),("k","d",2),("w","s"),("k","d",-2),),
+        (("q","z",2,1,3),("q","z",2,-1,3),("q","z",3,1,3),("q","z",3,-1,3),("q","y",3),("q","y",-3),("q","f",1),("k","f",3),("k","y",4),("q","d",2),("w","x",2),("w","x",1),("w","z",0,1,1),("w","z",0,-1,1),("q","d",-2),("q","f",2),("k","d",3),("q","f",3),("q","y",4),("k","d",-3),("w","z",2,1,1),("w","z",2,-1,1),("q","d",3),("w","x",3),("w","y",0),("w","z",1,1,1),("w","z",1,-1,1),("q","d",-3),("w","z",0,1,2),("w","z",0,-1,2),("k","d",4),),
+        (("w","z",2,1,2),("w","z",2,-1,2),),
+        (),
+        (),
+        (("w","z",3,1,1),("w","z",3,-1,1),("w","y",1),("w","y",-1),("q","d",4),("w","z",1,1,2),("w","z",1,-1,2),("w","z",0,1,3),("w","z",0,-1,3),("w","d",0),),
+        (("w","z",2,1,3),("w","z",2,-1,3),("w","z",3,1,2),("w","y",-2),("w","z",3,-1,2),("w","y",2),("w","z",1,1,3),("w","z",1,-1,3),("w","d",1),("w","f",0),("w","f",2),("w","d",-1),("w","z",3,1,3),("w","y",-3),("w","z",3,-1,3),("w","y",3),("w","f",1),("w","d",-2),),
+        (("w","f",3),("w","y",4),("w","d",2),),
+        (),
+        (),
+        (("w","d",-3),),
+        (("w","d",3),),
+        (("w","d",4),),
         (),
     ),
     (
-        (("q","y",0),("q","z",-1),("q","z",1),("q","y",-1),("q","z",2),("q","z",-2),("q","y",1),("q","r",0,-1),("q","r",0,1),("q","r",-1,-1),("q","r",-1,1),("q","y",2),("q","z",3),("q","z",-3),("q","y",-2),("w","s"),("q","r",1,-1),("q","r",1,1),("q","d",0),),
-        (("q","d",-1),("q","r",2,-1),("q","z",4),("w","z",-1),("q","y",3),("w","z",1),("q","y",-3),("w","y",0),("q","r",2,1),("q","r",-2,-1),("q","r",-2,1),("q","y",4),("q","d",1),("w","y",-1),("w","y",1),),
-        (("w","z",2),("w","z",-2),("q","r",3,-1),("q","r",-3,-1),("q","r",3,1),("w","r",0,-1),("q","r",-3,1),("w","r",0,1),("q","r",4,-1),("w","r",-1,-1),("q","d",2),("w","r",1,-1),("w","y",2),("w","y",-2),("q","d",-2),),
-        (("w","z",3),("w","z",-3),("q","r",4,1),("w","r",1,1),("w","r",-1,1),("q","d",3),("w","r",2,-1),("q","d",-3),("w","z",4),("w","d",0),("w","r",-2,-1),("w","r",2,1),("w","r",-2,1),("w","y",3),("w","y",-3),("q","d",4),),
-        (("w","d",1),("w","d",-1),("w","d",2),("w","r",3,-1),("w","d",-2),("w","r",3,1),("w","r",-3,-1),("w","r",-3,1),),
-        (("w","y",4),("w","d",3),("w","d",-3),("w","r",4,1),("w","r",4,-1),),
+        (("k","s"),("q","s"),),
+        (("k","z",1),("k","z",-1),("k","y",0),("q","y",0),("q","z",1),("k","y",1),("k","y",-1),("k","r",0,-1),("q","z",-1),("k","z",2),("k","z",-2),("q","r",0,-1),("k","r",0,1),("q","y",1),("k","r",1,-1),("k","r",-1,-1),("q","r",0,1),("k","r",1,1),("k","r",-1,1),("k","y",2),("k","y",-2),("k","z",3),("k","z",-3),("k","d",0),),
+        (("q","y",-1),("q","r",1,-1),("q","r",1,1),("q","d",0),("k","r",2,-1),("k","d",1),("k","r",-2,-1),("k","d",-1),("k","r",2,1),("k","y",3),("k","y",-3),("k","r",-2,1),("k","z",4),("q","z",2),("q","z",-2),("q","r",-1,-1),),
+        (("q","r",-1,1),("q","d",1),("k","d",2),("k","r",3,-1),("k","r",3,1),("k","r",-3,-1),("k","r",-3,1),("k","d",-2),("w","s"),("q","z",3),("q","z",-3),("k","y",4),("q","y",2),("q","y",-2),),
+        (("q","d",-1),("k","d",3),("k","d",-3),("w","z",-1),("w","z",1),("q","z",4),("k","r",4,-1),("k","r",4,1),("w","y",0),("w","z",2),("w","z",-2),("q","y",3),("q","y",-3),("q","r",2,1),("q","r",2,-1),("q","r",-2,1),("q","r",-2,-1),("k","d",4),("w","r",0,-1),("w","r",0,1),("w","z",3),("w","y",-1),("w","y",1),("w","z",-3),("q","y",4),("q","r",3,-1),("q","r",3,1),),
+        (("q","r",-3,1),("q","r",-3,-1),),
+        (("w","y",2),("w","y",-2),("q","d",2),),
+        (("q","d",-2),("w","d",0),),
+        (("w","r",-1,1),("w","r",-1,-1),("w","r",1,1),("w","r",1,-1),("w","z",4),("w","y",3),("w","y",-3),("q","r",4,-1),("q","r",4,1),),
+        (("q","d",3),("q","d",-3),("w","y",4),("w","r",2,-1),("w","r",2,1),("w","r",-2,-1),("w","r",-2,1),("w","d",-1),("w","d",1),("w","r",3,-1),("w","r",3,1),("w","r",-3,-1),("w","r",-3,1),("q","d",4),("w","r",4,-1),("w","r",4,1),),
+        (("w","d",2),),
+        (("w","d",-2),("w","d",3),("w","d",-3),),
+        (),
         (("w","d",4),),
-        (),
-        (),
         (),
         (),
         (),
@@ -61,8 +72,8 @@
 
 
 class Gather:
-    def __init__(self, direct, place, ssem, rsem, sib_r, slot, most):
-        self.direct, self.place = direct, place
+    def __init__(self, direct, relay, place, ssem, rsem, sib_r, slot, most):
+        self.direct, self.relay, self.place = direct, relay, place
         self.ssem, self.rsem, self.sib_r = ssem, rsem, sib_r
         self.slot, self.most = slot, most
         self.keys = ({}, {})
@@ -94,7 +105,7 @@
             self.copy(ref, self.sib_r.at[0], self.place.sibling()).wait_send()
 
     def a_s(self):
-        for step in (1, -1, 2):
+        for step in (1, -1) if self.relay else (1, -1, 2):
             self.send(0, (0, 0, 0, None), ("X", step), (0, 0, step))
         self.a_up(0)
 
@@ -104,6 +115,8 @@
 
     def a_x(self, j):
         self.recv(0, (0, 0, SIDE[j], None), ("X", -SIDE[j] if j < 3 else 2))
+        if self.relay and j < 3:
+            self.send(0, (0, 0, SIDE[j], j - 1), ("X", 2), (0, 0, -SIDE[j]))
         self.a_up(j)
 
     def a_z(self, j, way, s):
@@ -201,8 +214,8 @@
 
 
 def kernel(hid_hbm, seg_hbm, wq_hbm, wk_hbm, wv_hbm, wo_hbm, freq_ref, out_hbm,
-           hid, seg, qbuf, wbuf, wo_in, wo_sib, acc, cos_t, sin_t, bias, qrot, kvw, mixed, outv,
-           load_sem, out_sem, wo_s, wo_r, q_s, q_r, qs_r, w_s, w_r, ws_r,
+           hid, seg, kbuf, qbuf, wbuf, wo_in, wo_sib, acc, cos_t, sin_t, bias, qrot, kvw, mixed, outv,
+           load_sem, out_sem, wo_s, wo_r, k_s, k_r, ks_r, q_s, q_r, qs_r, w_s, w_r, ws_r,
            kv_s, kv_r, kvs_s, kvs_r):
     me = Place()
     c, k, i = me.c, me.k, me.ctx
@@ -211,13 +224,16 @@
         every = slice(None)
         return me.zi(zr), every if yr is None else me.yi(yr), every if xr is None else me.xi(xr)
 
-    def q_slot(core, zr, yr, xr, half):
-        rows = pl.ds(0, SHARD) if half is None else pl.ds(half * (SHARD // 2), SHARD // 2)
-        return qbuf.at[*chips(zr, yr, xr), core, rows, :]
-
-    def q_most(core):
-        return (qbuf.at[:, :, :, core], qbuf.at[0:NZ - 1, :, :, core],
-                qbuf.at[NZ - 1, 0, :, core], qbuf.at[NZ - 1, 1, 0:NX - 1, core])
+    def rows_of(buf):
+        def slot(core, zr, yr, xr, half):
+            rows = pl.ds(0, SHARD) if half is None else pl.ds(half * (SHARD // 2), SHARD // 2)
+            return buf.at[*chips(zr, yr, xr), core, rows, :]
+
+        def most(core):
+            return (buf.at[:, :, :, core], buf.at[0:NZ - 1, :, :, core],
+                    buf.at[NZ - 1, 0, :, core], buf.at[NZ - 1, 1, 0:NX - 1, core])
+
+        return slot, most
 
     def w_slot(core, zr, yr, xr, half):
         first, count = W_ROWS[core]
@@ -229,18 +245,19 @@
         return (wbuf.at[:, :, :, rows], wbuf.at[0:NZ - 1, :, :, rows],
                 wbuf.at[NZ - 1, 0, :, rows], wbuf.at[NZ - 1, 1, 0:NX - 1, rows])
 
-    gq = Gather(DIRECT[0], me, q_s, q_r, qs_r, q_slot, q_most)
-    gw = Gather(DIRECT[1], me, w_s, w_r, ws_r, w_slot, w_most)
+    gk = Gather(DIRECT[0], RELAY[0], me, k_s, k_r, ks_r, *rows_of(kbuf))
+    gq = Gather(DIRECT[1], RELAY[1], me, q_s, q_r, qs_r, *rows_of(qbuf))
+    gw = Gather(DIRECT[2], RELAY[2], me, w_s, w_r, ws_r, w_slot, w_most)
 
     def both(first, second):
         pl.when(c == 0)(first)
         pl.when(c == 1)(second)
 
-    own = qbuf.at[me.z, me.yl, me.x, c]
+    own_k, own_q = kbuf.at[me.z, me.yl, me.x, c], qbuf.at[me.z, me.yl, me.x, c]
     loads = [
-        pltpu.make_async_copy(wq_hbm, own.at[:, pl.ds(0, QW)], load_sem.at[0]),
-        pltpu.make_async_copy(wk_hbm, own.at[:, pl.ds(QW, HD)], load_sem.at[1]),
-        pltpu.make_async_copy(wv_hbm, own.at[:, pl.ds(QW + HD, HD)], load_sem.at[2]),
+        pltpu.make_async_copy(wk_hbm, own_k.at[:, pl.ds(0, HD)], load_sem.at[0]),
+        pltpu.make_async_copy(wv_hbm, own_k.at[:, pl.ds(HD, HD)], load_sem.at[1]),
+        pltpu.make_async_copy(wq_hbm, own_q, load_sem.at[2]),
         pltpu.make_async_copy(wo_hbm, wo_in, load_sem.at[3]),
         pltpu.make_async_copy(seg_hbm, seg, load_sem.at[4]),
         pltpu.make_async_copy(hid_hbm, hid, load_sem.at[5]),
@@ -272,7 +289,7 @@
     for load in loads[:3]:
         load.wait()
 
-    gathers = {"q": gq, "w": gw}
+    gathers = {"k": gk, "q": gq, "w": gw}
 
     def run(step):
         def core(which):
@@ -294,7 +311,7 @@
         block = jnp.concatenate(pair if core == 0 else pair[::-1], axis=0)
         wbuf[me.z, me.yl, me.x, rows, :] = jnp.transpose(block)
 
-    both(gq.a_s, gq.b_s)
+    run(0)
     loads[3].wait()
     wo_copy.start()
     row = lax.broadcasted_iota(jnp.int32, (BLOCK, HD), 0)
@@ -326,35 +343,31 @@
     loads[5].wait()
     acc[...] = jnp.zeros_like(acc)
 
-    def project(first, last):
+    part = NY * NX * 2 * SHARD
+    edges = (0, 1, 3, 5, 8)
+
+    def project(gather, buf, first, last, columns):
         @pl.loop(first, last)
         def _(t):
             zr = ((t + 1) // 2) * (2 * (t % 2) - 1)
             zz = (me.z + zr + NZ) % NZ
-            both(lambda: gq.sib_recv(1, zr), lambda: gq.sib_recv(0, zr))
-            part = NY * NX * 2 * SHARD
-            weights = qbuf[zz].reshape(part, QKV)
-            acc[...] += jnp.dot(hid[:, pl.ds(pl.multiple_of(zz * part, part), part)], weights,
-                                preferred_element_type=jnp.float32)
-
-    edges = (0, 1, 3, 5, 8)
+            both(lambda: gather.sib_recv(1, zr), lambda: gather.sib_recv(0, zr))
+            weights = buf[zz].reshape(part, buf.shape[-1])
+            acc[:, columns] += jnp.dot(hid[:, pl.ds(pl.multiple_of(zz * part, part), part)], weights,
+                                       preferred_element_type=jnp.float32)
+
+    def rotated(b, h):
+        piece = acc[b * BLOCK:(b + 1) * BLOCK, h * HD:(h + 1) * HD]
+        return (piece * cos_t[b] + pltpu.roll(piece, HD // 2, 1) * sin_t[b]).astype(jnp.bfloat16)
+
     for n in range(4):
-        run(n)
-        project(edges[n], edges[n + 1])
-    run(4)
-
+        run(1 + n)
+        project(gk, kbuf, edges[n], edges[n + 1], slice(QW, QKV))
+    run(5)
     for b in range(2):
-        rows = slice(b * BLOCK, (b + 1) * BLOCK)
         slot = REACH + c if b == 0 else c
-        for h in range(HQ + 1):
-            part = acc[rows, h * HD:(h + 1) * HD]
-            turned = part * cos_t[b] + pltpu.roll(part, HD // 2, 1) * sin_t[b]
-            turned = turned.astype(jnp.bfloat16)
-            if h < HQ:
-                qrot[b, h] = turned
-            else:
-                kvw[b, slot, :, 0:HD] = turned
-        kvw[b, slot, :, HD:2 * HD] = acc[rows, QW + HD:QKV].astype(jnp.bfloat16)
+        kvw[b, slot, :, 0:HD] = rotated(b, HQ)
+        kvw[b, slot, :, HD:2 * HD] = acc[b * BLOCK:(b + 1) * BLOCK, QW + HD:QKV].astype(jnp.bfloat16)
 
     def kv_copy(src, dst, sent, got, device):
         return pltpu.make_async_remote_copy(
@@ -383,7 +396,11 @@
     for b in range(2):
         kv_side(b, 0, c).start()
 
-    run(5)
+    for n in range(3):
+        run(6 + n)
+        project(gq, qbuf, edges[n], edges[n + 1], slice(0, QW))
+    run(9)
+
     for m in range(1, 5):
         def early_in(m=m):
             kv_copy(early_own, kvw.at[0, REACH - 2 * m + c], kv_s.at[0, m], kv_r.at[0, m], me.sibling()).wait_recv()
@@ -393,7 +410,13 @@
         kv_copy(late_own, kvw.at[1, 2 * m + c], kv_s.at[1, m], kv_r.at[1, m], me.sibling()).wait_recv()
         kv_side(1, m, c).start()
 
-    run(6)
+    run(10)
+    project(gq, qbuf, edges[3], edges[4], slice(0, QW))
+    run(11)
+    for b in range(2):
+        for h in range(HQ):
+            qrot[b, h] = rotated(b, h)
+    run(12)
 
     def attend(b):
         window = kvw.at[b, pl.ds(c, REACH + 1)]
@@ -418,10 +441,9 @@
         kv_side(1, m, 1 - c).wait_recv()
     attend(0)
 
-    run(7)
+    run(13)
     attend(1)
 
-    part = NY * NX * BLOCK
 
     def out_copy(t):
         zr = ((t + 1) // 2) * (2 * (t % 2) - 1)
@@ -442,10 +464,11 @@
         out_copy(t).start()
 
     for n in range(3):
-        run(8 + n)
+        run(14 + n)
         pl.loop(edges[n + 1] if n else 0, edges[n + 2])(emit)
 
     def finish(core):
+        gk.drain(core)
         gq.drain(core)
         gw.drain(core)
 
@@ -479,7 +502,8 @@
         scratch_shapes=[
             pltpu.VMEM((rows, D), bf16),
             pltpu.VMEM((4 * CHIPS, BLOCK), jnp.int32),
-            pltpu.VMEM((NZ, NY, NX, 2, SHARD, QKV), bf16),
+            pltpu.VMEM((NZ, NY, NX, 2, SHARD, 2 * HD), bf16),
+            pltpu.VMEM((NZ, NY, NX, 2, SHARD, QW), bf16),
             pltpu.VMEM((NZ, NY, NX, QW, BLOCK), bf16),
             pltpu.VMEM((SHARD, QW), bf16),
             pltpu.VMEM((SHARD, QW), bf16),
@@ -494,6 +518,7 @@
             dma((6,)), dma((NZ,)), dma, dma,
             dma, dma((40,)), dma((NZ,)),
             dma, dma((40,)), dma((NZ,)),
+            dma, dma((40,)), dma((NZ,)),
             dma((2, 5)), dma((2, 5)), dma((2, 5)), dma((2, 5)),
         ],
         compiler_params=pltpu.CompilerParams(

time: 82.2 us -> 77.5 us (0.943); the launches traced: 82.1 us -> 76.2 us
  Pallas kernels: 77.4 us -> 71.6 us
    pallas_call x1, Pallas kernels: 77.4 us -> 71.6 us  [on_device(): pl.pallas_call(kernel, out_shape=jax.ShapeDtypeStruct((rows, D), bf16), i...]
where the time goes in v3:
time: 77.5 us; the launch traced here: 76.2 us
  Pallas kernels  71.6 us (92%)
  local copies, waits for them, and re-layouts  4.64 us (6%)
    pallas_call x1, Pallas kernels, on_device(): pl.pallas_call(kernel, out_shape=jax.ShapeDtypeStruct((rows, D), bf16), i...  71.6 us
    unnamed x1, local copies, waits for them, and re-layouts  4.64 us

profile of v3, /device:TPU:9, one launch (start us, length us, event | category | flops | bytes accessed | tf_op | source)
XLA Modules:
  0.0 76.2 jit_solution(14931917038969457757)
XLA Ops:
  0.0 71.6 %layer.1 = bf16[256,8192]{1,0:T(8,128)(2,1)} custom-call(bf16[256,8192]{1,0:T(8,128)(2,1)} %hid_hbm.1, s32[256,128]{1,0:T(8,128)} %bitcast.2, bf16[64,512]{1,0:T(8,128)(2,1)} %wq_hbm.1, bf16[64,128]{1,0:T(8,128)(2,1)} %wk_hbm.1, bf16[64,128]{1,0:T(8,128)(2,1)} %wv_hbm.1, bf16[64,512]{1,0:T(8,128)(2,1)} %bitcast.3, f32[1,128]{1,0:T(1,128)} %constant.2.clone.freq_ref), custom_call_target="tpu_custom_call" | custom-call | tf_op jit(solution)/shard_map/layer/pallas_call | solution.py:497
  71.6 4.6 %copy.9 = bf16[256,8192]{1,0:T(8,128)(2,1)} copy(bf16[256,8192]{1,0:T(8,128)(2,1)} %layer.1) | data formatting | bytes 8388608

commit v4 on v3

--- a/solution.py
+++ b/solution.py
@@ -23,45 +23,46 @@
 SHARD = 64
 ORDER = (0, 1, -1, 2, -2, 3, -3, 4)
 FAR = -1e30
+FREQ = np.power(np.float32(ROPE_BASE), -np.arange(HD // 2, dtype=np.float32) * np.float32(2 / HD)).tolist()
 W_ROWS = ((0, 384), (384, 128))
 
 
 SIDE = (0, -1, 1, 2)
-DIRECT = (1, 2, 1)
+DIRECT = (3, 2, 1)
 RELAY = (False, False, True)
 PLAN = (
     (
         (("k","s"),("q","s"),),
-        (("k","x",1),("k","x",2),("k","z",0,1,1),("k","z",0,-1,1),("q","z",0,1,1),("q","z",0,-1,1),("q","x",1),("q","x",2),("k","x",3),("k","y",0),("k","z",1,1,1),("k","z",1,-1,1),("k","z",2,1,1),("k","z",2,-1,1),("k","z",0,1,2),("k","z",0,-1,2),("q","x",3),("q","y",0),("q","z",0,1,2),("q","z",0,-1,2),("k","d",0),("q","z",1,1,1),("q","z",1,-1,1),("k","z",3,1,1),("k","z",3,-1,1),("k","y",1),("k","y",-1),("k","z",1,1,2),("k","z",1,-1,2),("k","z",2,1,2),("k","z",2,-1,2),("k","z",0,1,3),("k","z",0,-1,3),("q","z",2,1,1),("q","z",2,-1,1),("q","d",0),("q","z",3,1,1),("q","z",3,-1,1),("q","y",1),),
-        (("q","z",0,1,3),("q","y",-1),("q","z",0,-1,3),("k","d",1),("q","z",1,1,2),("q","z",1,-1,2),("k","z",3,1,2),("k","z",3,-1,2),("k","y",2),("k","y",-2),("k","d",-1),("k","z",1,1,3),("k","z",1,-1,3),("k","z",2,1,3),("k","z",2,-1,3),),
-        (("k","f",0),("q","z",2,1,2),("q","z",2,-1,2),("q","z",3,1,2),("q","z",3,-1,2),("q","y",2),("q","y",-2),("q","d",1),("q","f",0),("q","z",1,1,3),("q","z",1,-1,3),("k","z",3,1,3),("k","z",3,-1,3),("k","y",3),("k","y",-3),("k","f",1),("k","f",2),("q","d",-1),("k","d",2),("w","s"),("k","d",-2),),
-        (("q","z",2,1,3),("q","z",2,-1,3),("q","z",3,1,3),("q","z",3,-1,3),("q","y",3),("q","y",-3),("q","f",1),("k","f",3),("k","y",4),("q","d",2),("w","x",2),("w","x",1),("w","z",0,1,1),("w","z",0,-1,1),("q","d",-2),("q","f",2),("k","d",3),("q","f",3),("q","y",4),("k","d",-3),("w","z",2,1,1),("w","z",2,-1,1),("q","d",3),("w","x",3),("w","y",0),("w","z",1,1,1),("w","z",1,-1,1),("q","d",-3),("w","z",0,1,2),("w","z",0,-1,2),("k","d",4),),
-        (("w","z",2,1,2),("w","z",2,-1,2),),
-        (),
-        (),
-        (("w","z",3,1,1),("w","z",3,-1,1),("w","y",1),("w","y",-1),("q","d",4),("w","z",1,1,2),("w","z",1,-1,2),("w","z",0,1,3),("w","z",0,-1,3),("w","d",0),),
-        (("w","z",2,1,3),("w","z",2,-1,3),("w","z",3,1,2),("w","y",-2),("w","z",3,-1,2),("w","y",2),("w","z",1,1,3),("w","z",1,-1,3),("w","d",1),("w","f",0),("w","f",2),("w","d",-1),("w","z",3,1,3),("w","y",-3),("w","z",3,-1,3),("w","y",3),("w","f",1),("w","d",-2),),
-        (("w","f",3),("w","y",4),("w","d",2),),
-        (),
-        (),
+        (("k","x",1),("k","x",2),("k","z",0,1,1),("k","z",0,-1,1),("q","z",0,1,1),("q","z",0,-1,1),("q","x",1),("k","x",3),("k","y",0),("q","x",2),("k","z",1,1,1),("k","z",1,-1,1),("q","x",3),("q","y",0),("k","z",2,1,1),("k","z",2,-1,1),("k","z",0,1,2),("k","z",0,-1,2),("q","z",0,1,2),("k","d",0),("q","z",0,-1,2),("q","z",1,1,1),("k","z",3,1,1),("k","z",3,-1,1),("k","y",1),("k","y",-1),("q","z",1,-1,1),("q","z",2,1,1),("k","z",1,1,2),("k","z",1,-1,2),("q","z",2,-1,1),("q","z",3,1,1),("q","y",-1),("q","d",0),),
+        (("k","z",2,1,2),("k","z",0,1,3),("q","z",3,-1,1),("q","y",1),("k","z",2,-1,2),("k","z",0,-1,3),("q","z",0,1,3),("w","s"),("k","d",1),("k","z",3,1,2),("k","z",3,-1,2),("k","y",2),("k","y",-2),("k","d",-1),("q","z",1,1,2),("q","z",1,-1,2),("k","z",1,1,3),("k","z",1,-1,3),("q","z",2,1,2),),
+        (("k","z",2,1,3),("q","z",2,-1,2),("q","d",-1),("k","z",2,-1,3),("q","z",3,1,2),("k","f",0),("q","z",3,-1,2),("q","y",2),("q","d",1),("w","z",0,1,1),("q","z",0,-1,3),("q","y",-2),("k","d",2),("k","z",3,1,3),("k","y",-3),("w","x",1),("k","z",3,-1,3),("k","y",3),("w","x",2),("k","d",-2),("w","z",0,-1,1),("q","z",1,1,3),("q","z",1,-1,3),("k","f",1),("q","z",2,1,3),("q","z",2,-1,3),),
+        (("k","f",2),("q","z",3,1,3),("q","z",3,-1,3),("q","y",3),("q","y",-3),("q","d",2),("q","f",0),("w","z",0,1,2),("w","z",1,-1,1),("q","d",-2),("k","f",3),("k","y",4),("k","d",-3),("w","x",3),("w","y",0),("w","z",1,1,1),("w","z",2,-1,1),("k","d",3),("w","z",2,1,1),("w","z",0,-1,2),("q","f",1),("q","f",2),("q","d",3),("q","f",3),("q","y",4),("q","d",-3),("w","z",0,1,3),("w","z",1,-1,2),("k","d",4),("w","z",3,1,1),("w","z",3,-1,1),("w","y",1),("w","y",-1),),
+        (("w","z",1,1,2),("w","z",2,-1,2),),
+        (("w","d",0),("w","z",2,1,2),("w","z",0,-1,3),),
+        (),
+        (("w","z",1,-1,3),("q","d",4),),
+        (("w","z",3,1,2),("w","z",3,-1,2),("w","y",2),("w","y",-2),("w","z",1,1,3),("w","z",2,-1,3),("w","f",0),("w","d",1),("w","z",2,1,3),("w","d",-1),("w","z",3,1,3),("w","z",3,-1,3),("w","y",3),("w","y",-3),("w","f",1),("w","f",2),("w","d",2),("w","f",3),("w","y",4),("w","d",-2),),
+        (),
+        (),
+        (("w","d",3),),
         (("w","d",-3),),
-        (("w","d",3),),
         (("w","d",4),),
+        (),
         (),
     ),
     (
         (("k","s"),("q","s"),),
-        (("k","z",1),("k","z",-1),("k","y",0),("q","y",0),("q","z",1),("k","y",1),("k","y",-1),("k","r",0,-1),("q","z",-1),("k","z",2),("k","z",-2),("q","r",0,-1),("k","r",0,1),("q","y",1),("k","r",1,-1),("k","r",-1,-1),("q","r",0,1),("k","r",1,1),("k","r",-1,1),("k","y",2),("k","y",-2),("k","z",3),("k","z",-3),("k","d",0),),
-        (("q","y",-1),("q","r",1,-1),("q","r",1,1),("q","d",0),("k","r",2,-1),("k","d",1),("k","r",-2,-1),("k","d",-1),("k","r",2,1),("k","y",3),("k","y",-3),("k","r",-2,1),("k","z",4),("q","z",2),("q","z",-2),("q","r",-1,-1),),
-        (("q","r",-1,1),("q","d",1),("k","d",2),("k","r",3,-1),("k","r",3,1),("k","r",-3,-1),("k","r",-3,1),("k","d",-2),("w","s"),("q","z",3),("q","z",-3),("k","y",4),("q","y",2),("q","y",-2),),
-        (("q","d",-1),("k","d",3),("k","d",-3),("w","z",-1),("w","z",1),("q","z",4),("k","r",4,-1),("k","r",4,1),("w","y",0),("w","z",2),("w","z",-2),("q","y",3),("q","y",-3),("q","r",2,1),("q","r",2,-1),("q","r",-2,1),("q","r",-2,-1),("k","d",4),("w","r",0,-1),("w","r",0,1),("w","z",3),("w","y",-1),("w","y",1),("w","z",-3),("q","y",4),("q","r",3,-1),("q","r",3,1),),
+        (("k","z",-1),("k","z",1),("k","y",0),("q","y",0),("q","z",-1),("q","z",1),("k","y",-1),("k","z",-2),("k","z",2),("k","y",1),("k","r",0,-1),("k","r",0,1),("q","z",2),("q","r",0,1),("q","r",0,-1),("k","z",-3),("k","z",3),("q","y",1),("k","y",-2),("k","y",2),("k","r",-1,1),("k","r",-1,-1),("k","r",1,1),("k","r",1,-1),("k","d",0),),
+        (("q","y",-1),("q","y",2),("k","y",-3),("k","y",3),("q","d",0),("k","z",4),("w","s"),("k","r",-2,1),("k","r",-2,-1),("k","r",2,1),("k","r",2,-1),("k","d",-1),("k","d",1),("q","z",-2),),
+        (("q","z",3),("k","r",-3,1),("k","r",-3,-1),("k","r",3,1),("k","r",3,-1),("w","z",-1),("w","z",1),("k","y",4),("w","y",0),("q","r",1,1),("q","r",1,-1),("k","d",-2),("q","r",-1,1),("q","r",-1,-1),("k","d",2),("q","y",-2),("q","r",2,1),("q","y",3),("q","r",2,-1),),
+        (("q","z",-3),("k","d",-3),("k","d",3),("w","y",-1),("w","z",2),("w","z",-2),("k","r",4,1),("k","r",4,-1),("w","y",1),("w","r",0,1),("w","r",0,-1),("q","d",1),("q","d",-1),("q","y",-3),("q","r",-2,1),("q","r",-2,-1),("q","r",3,-1),("q","z",4),("q","r",3,1),("w","z",3),("w","z",-3),("q","d",2),("w","r",-1,1),("w","r",-1,-1),("w","y",2),("w","y",-2),("k","d",4),("w","r",1,1),("w","r",1,-1),("w","d",0),),
         (("q","r",-3,1),("q","r",-3,-1),),
-        (("w","y",2),("w","y",-2),("q","d",2),),
-        (("q","d",-2),("w","d",0),),
-        (("w","r",-1,1),("w","r",-1,-1),("w","r",1,1),("w","r",1,-1),("w","z",4),("w","y",3),("w","y",-3),("q","r",4,-1),("q","r",4,1),),
-        (("q","d",3),("q","d",-3),("w","y",4),("w","r",2,-1),("w","r",2,1),("w","r",-2,-1),("w","r",-2,1),("w","d",-1),("w","d",1),("w","r",3,-1),("w","r",3,1),("w","r",-3,-1),("w","r",-3,1),("q","d",4),("w","r",4,-1),("w","r",4,1),),
-        (("w","d",2),),
-        (("w","d",-2),("w","d",3),("w","d",-3),),
+        (("w","z",4),("q","y",4),("q","d",-2),),
+        (),
+        (("q","d",3),("w","y",3),("w","y",-3),),
+        (("w","r",2,1),("w","r",2,-1),("w","r",-2,1),("w","r",-2,-1),("w","d",1),("w","d",-1),("q","d",-3),("w","y",4),("q","r",4,1),("q","r",4,-1),("w","r",3,1),("w","r",3,-1),("w","r",-3,1),("w","r",-3,-1),("w","d",2),("w","d",-2),("w","r",4,1),("w","r",4,-1),("q","d",4),),
+        (("w","d",3),),
+        (("w","d",-3),),
         (),
         (("w","d",4),),
         (),
@@ -213,7 +214,7 @@
         return {"ctx": chip * 2 + core, "dp": self.dp}
 
 
-def kernel(hid_hbm, seg_hbm, wq_hbm, wk_hbm, wv_hbm, wo_hbm, freq_ref, out_hbm,
+def kernel(hid_hbm, seg_hbm, packed, out_hbm,
            hid, seg, kbuf, qbuf, wbuf, wo_in, wo_sib, acc, cos_t, sin_t, bias, qrot, kvw, mixed, outv,
            load_sem, out_sem, wo_s, wo_r, k_s, k_r, ks_r, q_s, q_r, qs_r, w_s, w_r, ws_r,
            kv_s, kv_r, kvs_s, kvs_r):
@@ -255,12 +256,11 @@
 
     own_k, own_q = kbuf.at[me.z, me.yl, me.x, c], qbuf.at[me.z, me.yl, me.x, c]
     loads = [
-        pltpu.make_async_copy(wk_hbm, own_k.at[:, pl.ds(0, HD)], load_sem.at[0]),
-        pltpu.make_async_copy(wv_hbm, own_k.at[:, pl.ds(HD, HD)], load_sem.at[1]),
-        pltpu.make_async_copy(wq_hbm, own_q, load_sem.at[2]),
-        pltpu.make_async_copy(wo_hbm, wo_in, load_sem.at[3]),
-        pltpu.make_async_copy(seg_hbm, seg, load_sem.at[4]),
-        pltpu.make_async_copy(hid_hbm, hid, load_sem.at[5]),
+        pltpu.make_async_copy(packed.at[:, pl.ds(0, 2 * HD)], own_k, load_sem.at[0]),
+        pltpu.make_async_copy(packed.at[:, pl.ds(2 * HD, QW)], own_q, load_sem.at[1]),
+        pltpu.make_async_copy(packed.at[:, pl.ds(QKV, QW)], wo_in, load_sem.at[2]),
+        pltpu.make_async_copy(seg_hbm, seg, load_sem.at[3]),
+        pltpu.make_async_copy(hid_hbm, hid, load_sem.at[4]),
     ]
     for load in loads:
         load.start()
@@ -286,7 +286,7 @@
         pl.when(k >= m)(lambda m=m: greet(me.on(k - m, c)))
     pl.semaphore_wait(barrier, len(moves) + 5 + jnp.minimum(k, 4))
 
-    for load in loads[:3]:
+    for load in loads[:2]:
         load.wait()
 
     gathers = {"k": gk, "q": gq, "w": gw}
@@ -312,18 +312,22 @@
         wbuf[me.z, me.yl, me.x, rows, :] = jnp.transpose(block)
 
     run(0)
-    loads[3].wait()
+    loads[2].wait()
     wo_copy.start()
+    wave = lax.broadcasted_iota(jnp.int32, (1, HD), 1) % (HD // 2)
+    freq = jnp.zeros((1, HD), jnp.float32)
+    for j in range(HD // 2):
+        freq = jnp.where(wave == j, FREQ[j], freq)
     row = lax.broadcasted_iota(jnp.int32, (BLOCK, HD), 0)
     lane = lax.broadcasted_iota(jnp.int32, (BLOCK, HD), 1)
     late = 2 * 2 * CHIPS - 1 - i
     for b, block in enumerate((i, late)):
-        angle = (block * BLOCK + row).astype(jnp.float32) * freq_ref[...]
+        angle = (block * BLOCK + row).astype(jnp.float32) * freq
         cos_t[b] = jnp.cos(angle)
         sine = jnp.sin(angle)
         sin_t[b] = jnp.where(lane < HD // 2, -sine, sine)
 
-    loads[4].wait()
+    loads[3].wait()
     for b in range(2):
         mine = seg[pl.ds(2 * i + b, 1), :]
         asks = jnp.transpose(jnp.broadcast_to(mine, (BLOCK, BLOCK)))
@@ -340,7 +344,7 @@
                 allowed = allowed & (lane <= row)
             bias[b, :, j * BLOCK:(j + 1) * BLOCK] = jnp.where(allowed, 0.0, FAR)
 
-    loads[5].wait()
+    loads[4].wait()
     acc[...] = jnp.zeros_like(acc)
 
     part = NY * NX * 2 * SHARD
@@ -431,8 +435,8 @@
         peak = jnp.max(scores, axis=1, keepdims=True)
         terms = jnp.exp2(scores - peak)
         total = jnp.sum(terms, axis=1, keepdims=True)
-        weights = (terms * (1.0 / total)).astype(jnp.bfloat16)
-        result = jnp.dot(weights, values, preferred_element_type=jnp.float32).astype(jnp.bfloat16)
+        result = jnp.dot(terms.astype(jnp.bfloat16), values, preferred_element_type=jnp.float32)
+        result = (result * (1.0 / total)).astype(jnp.bfloat16)
         for h in range(HQ):
             mixed[b * BLOCK:(b + 1) * BLOCK, h * HD:(h + 1) * HD] = result[h * BLOCK:(h + 1) * BLOCK]
 
@@ -486,9 +490,6 @@
 
 
 def on_device(hidden_in, segment_ids, w_query, w_key, w_value, w_out):
-    half = np.arange(HD // 2, dtype=np.float32) * np.float32(2.0) / np.float32(HD)
-    freq = np.power(np.float32(ROPE_BASE), -half).astype(np.float32)
-    freq = jnp.asarray(np.concatenate([freq, freq])[None, :])
     seg = segment_ids.reshape(4 * CHIPS, BLOCK)
     rows = hidden_in.shape[0]
     anywhere = pl.BlockSpec(memory_space=pl.ANY)
@@ -497,7 +498,7 @@
     return pl.pallas_call(
         kernel,
         out_shape=jax.ShapeDtypeStruct((rows, D), bf16),
-        in_specs=[anywhere] * 6 + [pl.BlockSpec(memory_space=pltpu.VMEM)],
+        in_specs=[anywhere] * 3,
         out_specs=anywhere,
         scratch_shapes=[
             pltpu.VMEM((rows, D), bf16),
@@ -515,16 +516,16 @@
             pltpu.VMEM((2, REACH + 2, BLOCK, 2 * HD), bf16),
             pltpu.VMEM((rows, QW), bf16),
             pltpu.VMEM((rows, D), bf16),
-            dma((6,)), dma((NZ,)), dma, dma,
+            dma((5,)), dma((NZ,)), dma, dma,
             dma, dma((40,)), dma((NZ,)),
             dma, dma((40,)), dma((NZ,)),
             dma, dma((40,)), dma((NZ,)),
             dma((2, 5)), dma((2, 5)), dma((2, 5)), dma((2, 5)),
         ],
         compiler_params=pltpu.CompilerParams(
-            collective_id=1, has_side_effects=True, vmem_limit_bytes=60 * 2**20),
+            collective_id=1, has_side_effects=True, vmem_limit_bytes=48 * 2**20),
         name="layer",
-    )(hidden_in, seg, w_query, w_key, w_value, w_out.T, freq)
+    )(hidden_in, seg, jnp.concatenate([w_key, w_value, w_query, w_out.T], axis=1))
 
 
 def solution(mesh):

time: 77.5 us -> 74.2 us (0.957)
  Pallas kernels: 71.6 us -> 69.7 us
  local copies, waits for them, and re-layouts: 4.64 us -> 2.92 us
  other arithmetic: 0 us -> 0.89 us
    pallas_call x1, Pallas kernels: 71.6 us -> 69.7 us  [on_device(): pl.pallas_call(kernel, out_shape=jax.ShapeDtypeStruct((rows, D), bf16), i...]
    unnamed x1 -> x3, local copies, waits for them, and re-layouts: 4.64 us -> 2.92 us
    concatenate x0 -> x1, other arithmetic: none -> 0.89 us  [on_device(): jnp.concatenate([w_key, w_value, w_query, w_out.T], axis=1)]
where the time goes in v4:
time: 74.2 us; the launch traced here: 73.5 us
  Pallas kernels  69.7 us (94%)
  local copies, waits for them, and re-layouts  2.92 us (4%)
  other arithmetic  0.89 us (1%)
    pallas_call x1, Pallas kernels, on_device(): pl.pallas_call(kernel, out_shape=jax.ShapeDtypeStruct((rows, D), bf16), i...  69.7 us
    unnamed x3, local copies, waits for them, and re-layouts  2.92 us

profile of v4, /device:TPU:9, one launch (start us, length us, event | category | flops | bytes accessed | tf_op | source)
XLA Modules:
  0.0 73.5 jit_solution(10849454410691588700)
XLA Ops:
  0.0 0.9 %pad_maximum_fusion.packed = bf16[64,1280]{1,0:T(8,128)(2,1)S(1)} fusion(bf16[64,512]{1,0:T(8,128)(2,1)} %bitcast.3, bf16[64,512]{1,0:T(8,128)(2,1)} %param.8, bf16[64,128]{1,0:T(8,128)(2,1)} %param.10, bf16[64,128]{1,0:T(8,128)(2,1)} %param.9), kind=kLoop, calls=%fused_computation | loop fusion | flops 655360 | bytes 327680 | tf_op jit(solution)/shard_map/concatenate | solution.py:528
  0.9 0.0 copy-start
  0.9 0.9 %copy-done = s32[32768]{0:T(1024)S(1)} copy-done((s32[32768]{0:T(1024)S(1)}, s32[32768]{0:T(1024)}, u32[]{:S(2)}) %copy-start) | copy-done | bytes 131096
  1.8 69.7 %layer.1 = bf16[256,8192]{1,0:T(8,128)(2,1)S(1)} custom-call(bf16[256,8192]{1,0:T(8,128)(2,1)} %hid_hbm.1, s32[256,128]{1,0:T(8,128)S(1)} %bitcast.2, bf16[64,1280]{1,0:T(8,128)(2,1)S(1)} %pad_maximum_fusion.packed), custom_call_target="tpu_custom_call" | custom-call | tf_op jit(solution)/shard_map/layer/pallas_call | solution.py:498
  71.5 2.0 %copy.8 = bf16[256,8192]{1,0:T(8,128)(2,1)} copy(bf16[256,8192]{1,0:T(8,128)(2,1)S(1)} %layer.1) | data formatting | bytes 8388608
Async XLA Ops:
  0.9 0.9 %copy-start = (s32[32768]{0:T(1024)S(1)}, s32[32768]{0:T(1024)}, u32[]{:S(2)}) copy-start(s32[32768]{0:T(1024)} %param.7) | copy-start | bytes 393220

commit v5 on v4

--- a/solution.py
+++ b/solution.py
@@ -28,44 +28,45 @@
 
 
 SIDE = (0, -1, 1, 2)
-DIRECT = (3, 2, 1)
-RELAY = (False, False, True)
+DIRECT = (1, 2, 1)
+RELAY = (True, True, True)
+Y_FIRST = (False, False, True)
 PLAN = (
     (
         (("k","s"),("q","s"),),
-        (("k","x",1),("k","x",2),("k","z",0,1,1),("k","z",0,-1,1),("q","z",0,1,1),("q","z",0,-1,1),("q","x",1),("k","x",3),("k","y",0),("q","x",2),("k","z",1,1,1),("k","z",1,-1,1),("q","x",3),("q","y",0),("k","z",2,1,1),("k","z",2,-1,1),("k","z",0,1,2),("k","z",0,-1,2),("q","z",0,1,2),("k","d",0),("q","z",0,-1,2),("q","z",1,1,1),("k","z",3,1,1),("k","z",3,-1,1),("k","y",1),("k","y",-1),("q","z",1,-1,1),("q","z",2,1,1),("k","z",1,1,2),("k","z",1,-1,2),("q","z",2,-1,1),("q","z",3,1,1),("q","y",-1),("q","d",0),),
-        (("k","z",2,1,2),("k","z",0,1,3),("q","z",3,-1,1),("q","y",1),("k","z",2,-1,2),("k","z",0,-1,3),("q","z",0,1,3),("w","s"),("k","d",1),("k","z",3,1,2),("k","z",3,-1,2),("k","y",2),("k","y",-2),("k","d",-1),("q","z",1,1,2),("q","z",1,-1,2),("k","z",1,1,3),("k","z",1,-1,3),("q","z",2,1,2),),
-        (("k","z",2,1,3),("q","z",2,-1,2),("q","d",-1),("k","z",2,-1,3),("q","z",3,1,2),("k","f",0),("q","z",3,-1,2),("q","y",2),("q","d",1),("w","z",0,1,1),("q","z",0,-1,3),("q","y",-2),("k","d",2),("k","z",3,1,3),("k","y",-3),("w","x",1),("k","z",3,-1,3),("k","y",3),("w","x",2),("k","d",-2),("w","z",0,-1,1),("q","z",1,1,3),("q","z",1,-1,3),("k","f",1),("q","z",2,1,3),("q","z",2,-1,3),),
-        (("k","f",2),("q","z",3,1,3),("q","z",3,-1,3),("q","y",3),("q","y",-3),("q","d",2),("q","f",0),("w","z",0,1,2),("w","z",1,-1,1),("q","d",-2),("k","f",3),("k","y",4),("k","d",-3),("w","x",3),("w","y",0),("w","z",1,1,1),("w","z",2,-1,1),("k","d",3),("w","z",2,1,1),("w","z",0,-1,2),("q","f",1),("q","f",2),("q","d",3),("q","f",3),("q","y",4),("q","d",-3),("w","z",0,1,3),("w","z",1,-1,2),("k","d",4),("w","z",3,1,1),("w","z",3,-1,1),("w","y",1),("w","y",-1),),
-        (("w","z",1,1,2),("w","z",2,-1,2),),
-        (("w","d",0),("w","z",2,1,2),("w","z",0,-1,3),),
-        (),
-        (("w","z",1,-1,3),("q","d",4),),
-        (("w","z",3,1,2),("w","z",3,-1,2),("w","y",2),("w","y",-2),("w","z",1,1,3),("w","z",2,-1,3),("w","f",0),("w","d",1),("w","z",2,1,3),("w","d",-1),("w","z",3,1,3),("w","z",3,-1,3),("w","y",3),("w","y",-3),("w","f",1),("w","f",2),("w","d",2),("w","f",3),("w","y",4),("w","d",-2),),
-        (),
-        (),
+        (("k","x",1),("k","x",2),("k","z",0,1,1),("k","z",0,-1,1),("q","x",1),("q","x",2),("q","z",0,1,1),("q","z",0,-1,1),("k","z",1,1,1),("k","z",1,-1,1),("k","x",3),("k","y",0),("k","z",2,1,1),("k","z",2,-1,1),("k","z",0,1,2),("k","z",0,-1,2),("q","z",1,1,1),("q","z",1,-1,1),("q","x",3),("q","y",0),("q","z",2,1,1),("q","z",2,-1,1),("k","z",1,-1,2),("q","z",0,1,2),("k","z",3,-1,1),("k","y",1),("k","d",0),("k","z",1,1,2),("k","z",2,-1,2),("k","z",3,1,1),("k","y",-1),("k","z",0,-1,3),("k","z",2,1,2),("k","z",0,1,3),("q","z",0,-1,2),),
+        (("q","z",1,-1,2),("q","z",1,1,2),("q","z",3,-1,1),("q","y",1),("q","z",3,1,1),("q","d",0),("q","z",2,1,2),("w","s"),("q","y",-1),("k","d",1),("k","z",1,-1,3),("k","z",3,-1,2),("k","y",2),("k","z",1,1,3),("k","d",-1),("k","z",2,-1,3),("k","z",3,1,2),("k","y",-2),("k","z",2,1,3),("q","z",2,-1,2),("k","f",0),("q","z",0,-1,3),("q","z",0,1,3),("q","z",1,-1,3),("q","z",1,1,3),("q","d",1),("q","z",3,-1,2),("q","y",2),),
+        (("q","z",3,1,2),("q","z",2,1,3),("w","z",0,-1,1),("q","y",-2),("w","x",1),("w","x",2),("k","z",3,-1,3),("k","y",3),("w","z",0,1,1),("q","d",-1),("k","f",1),("k","d",2),("q","z",2,-1,3),("k","z",3,1,3),("k","y",-3),("k","f",2),("k","d",-2),("q","f",0),("q","f",1),("q","z",3,-1,3),("q","y",3),("q","z",3,1,3),("q","y",-3),),
+        (("q","d",2),("w","z",0,-1,2),("w","z",1,1,1),("q","d",-2),("w","z",1,-1,1),("w","x",3),("k","d",3),("w","y",0),("w","z",2,1,1),("w","z",2,-1,1),("k","d",-3),("w","z",0,1,2),("k","f",3),("k","y",4),("q","f",2),("q","f",3),("q","y",4),("q","d",3),("w","z",1,1,2),("w","z",0,-1,3),("q","d",-3),("w","z",3,1,1),("w","y",-1),("w","z",1,-1,2),("w","z",2,1,2),("w","z",3,-1,1),("w","y",1),("w","d",0),("w","z",0,1,3),("w","z",2,-1,2),("k","d",4),("w","z",1,1,3),("q","d",4),),
+        (("w","z",3,1,2),("w","y",-2),("w","z",1,-1,3),),
+        (("w","z",3,-1,2),("w","y",2),("w","d",-1),("w","z",2,1,3),),
+        (),
+        (("w","z",2,-1,3),("w","f",0),),
+        (("w","d",1),("w","f",1),("w","z",3,1,3),("w","y",-3),("w","z",3,-1,3),("w","y",3),("w","d",-2),("w","f",2),("w","d",2),("w","f",3),("w","y",4),),
+        (),
+        (),
+        (("w","d",-3),),
         (("w","d",3),),
-        (("w","d",-3),),
         (("w","d",4),),
         (),
         (),
     ),
     (
         (("k","s"),("q","s"),),
-        (("k","z",-1),("k","z",1),("k","y",0),("q","y",0),("q","z",-1),("q","z",1),("k","y",-1),("k","z",-2),("k","z",2),("k","y",1),("k","r",0,-1),("k","r",0,1),("q","z",2),("q","r",0,1),("q","r",0,-1),("k","z",-3),("k","z",3),("q","y",1),("k","y",-2),("k","y",2),("k","r",-1,1),("k","r",-1,-1),("k","r",1,1),("k","r",1,-1),("k","d",0),),
-        (("q","y",-1),("q","y",2),("k","y",-3),("k","y",3),("q","d",0),("k","z",4),("w","s"),("k","r",-2,1),("k","r",-2,-1),("k","r",2,1),("k","r",2,-1),("k","d",-1),("k","d",1),("q","z",-2),),
-        (("q","z",3),("k","r",-3,1),("k","r",-3,-1),("k","r",3,1),("k","r",3,-1),("w","z",-1),("w","z",1),("k","y",4),("w","y",0),("q","r",1,1),("q","r",1,-1),("k","d",-2),("q","r",-1,1),("q","r",-1,-1),("k","d",2),("q","y",-2),("q","r",2,1),("q","y",3),("q","r",2,-1),),
-        (("q","z",-3),("k","d",-3),("k","d",3),("w","y",-1),("w","z",2),("w","z",-2),("k","r",4,1),("k","r",4,-1),("w","y",1),("w","r",0,1),("w","r",0,-1),("q","d",1),("q","d",-1),("q","y",-3),("q","r",-2,1),("q","r",-2,-1),("q","r",3,-1),("q","z",4),("q","r",3,1),("w","z",3),("w","z",-3),("q","d",2),("w","r",-1,1),("w","r",-1,-1),("w","y",2),("w","y",-2),("k","d",4),("w","r",1,1),("w","r",1,-1),("w","d",0),),
-        (("q","r",-3,1),("q","r",-3,-1),),
-        (("w","z",4),("q","y",4),("q","d",-2),),
-        (),
-        (("q","d",3),("w","y",3),("w","y",-3),),
-        (("w","r",2,1),("w","r",2,-1),("w","r",-2,1),("w","r",-2,-1),("w","d",1),("w","d",-1),("q","d",-3),("w","y",4),("q","r",4,1),("q","r",4,-1),("w","r",3,1),("w","r",3,-1),("w","r",-3,1),("w","r",-3,-1),("w","d",2),("w","d",-2),("w","r",4,1),("w","r",4,-1),("q","d",4),),
+        (("k","y",0),("k","z",-1),("k","z",1),("q","y",0),("q","z",-1),("q","z",1),("q","z",-2),("k","r",0,-1),("k","r",0,1),("k","y",-1),("k","y",1),("k","z",-2),("k","z",2),("q","r",0,1),("q","r",0,-1),("q","z",2),("q","y",1),("q","y",-1),("k","d",0),("k","y",-2),("k","r",-1,1),("k","y",2),("k","z",3),("k","r",1,1),("k","r",1,-1),("k","r",-1,-1),("k","z",-3),),
+        (("q","d",0),("q","z",-3),("q","y",2),("w","s"),("k","r",-2,1),("k","r",-2,-1),("k","y",3),("k","y",-3),("k","r",2,-1),("k","r",2,1),("k","z",4),("k","d",1),("k","d",-1),),
+        (("q","r",1,1),("q","r",1,-1),("q","r",-1,1),("q","r",-1,-1),("q","r",2,1),("w","v",1,0),("q","r",2,-1),("w","y",0),("w","p",0),("q","z",3),("w","v",-1,0),("k","d",-2),("k","r",3,1),("k","r",3,-1),("q","y",-2),("k","r",-3,1),("k","r",-3,-1),("k","y",4),("k","d",2),("q","y",-3),),
+        (("q","d",1),("q","d",-1),("w","v",2,0),("q","d",2),("w","r",0,1),("w","r",0,-1),("w","v",-1,1),("w","p",-1),("q","y",3),("w","v",1,1),("w","p",1),("q","z",4),("k","d",3),("w","v",-2,0),("q","r",-2,1),("q","r",-2,-1),("k","d",-3),("k","r",4,1),("k","r",4,-1),("q","r",-3,1),("w","v",3,0),("q","r",-3,-1),("w","d",0),("w","r",-1,1),("w","r",-1,-1),("q","r",3,1),("q","r",3,-1),("w","r",1,1),("w","v",-2,1),("w","r",1,-1),("w","p",-2),("q","y",4),("w","v",-3,0),("w","v",2,1),("w","p",2),("q","d",-2),("k","d",4),),
+        (),
+        (("w","d",-1),("q","d",-3),),
+        (),
+        (("w","r",-2,-1),("w","v",-3,1),("w","r",-2,1),("w","d",1),("w","p",-3),("q","d",3),("q","r",4,1),("w","v",3,1),("w","v",4,0),("w","p",3),("q","r",4,-1),),
+        (("w","r",2,1),("w","r",2,-1),("w","v",4,1),("w","p",4),("w","r",-3,1),("w","r",-3,-1),("w","d",-2),("w","r",3,-1),),
+        (("w","r",3,1),("q","d",4),),
+        (("w","d",2),),
+        (("w","r",4,1),("w","r",4,-1),("w","d",-3),),
         (("w","d",3),),
-        (("w","d",-3),),
-        (),
         (("w","d",4),),
-        (),
         (),
         (),
     ),
@@ -73,8 +74,8 @@
 
 
 class Gather:
-    def __init__(self, direct, relay, place, ssem, rsem, sib_r, slot, most):
-        self.direct, self.relay, self.place = direct, relay, place
+    def __init__(self, direct, relay, y_first, place, ssem, rsem, sib_r, slot, most):
+        self.direct, self.relay, self.y_first, self.place = direct, relay, y_first, place
         self.ssem, self.rsem, self.sib_r = ssem, rsem, sib_r
         self.slot, self.most = slot, most
         self.keys = ({}, {})
@@ -141,10 +142,13 @@
 
     def b_s(self):
         self.b_fan(0, 0)
+        self.b_up(0)
+        self.b_cross(0)
+
+    def b_up(self, yr):
         for far in range(1, self.direct + 1):
             for way in (1, -1):
-                self.send(1, (0, 0, 0, None), ("Z", way, far), (way * far, 0, 0))
-        self.b_cross(0)
+                self.send(1, (0, yr, 0, None), ("Z", way, far, yr), (way * far, 0, 0))
 
     def b_fan(self, zr, yr):
         for way in (1, -1):
@@ -154,22 +158,31 @@
         for way in (1, -1):
             self.send(1, (zr, 0, 0, (1 - way) // 2), ("Y", zr), (0, way, 0))
 
-    def b_z(self, zr):
+    def b_v(self, zr, yr):
         if zr == 4:
-            self.recv(1, (4, 0, 0, None), ("Z", 4))
+            self.recv(1, (4, yr, 0, None), ("Z", 4, yr))
         else:
             way, far = (-1 if zr > 0 else 1), abs(zr)
-            self.recv(1, (zr, 0, 0, None), ("Z", way, far))
+            self.recv(1, (zr, yr, 0, None), ("Z", way, far, yr))
             if far == 3:
-                self.send(1, (zr, 0, 0, (1 - way) // 2), ("Z", 4), (way, 0, 0))
+                self.send(1, (zr, yr, 0, (1 - way) // 2), ("Z", 4, yr), (way, 0, 0))
             elif far + 1 > self.direct:
-                self.send(1, (zr, 0, 0, None), ("Z", way, far + 1), (way, 0, 0))
-        self.b_fan(zr, 0)
+                self.send(1, (zr, yr, 0, None), ("Z", way, far + 1, yr), (way, 0, 0))
+        self.b_fan(zr, yr)
+
+    def b_z(self, zr):
+        self.b_v(zr, 0)
         self.b_cross(zr)
 
     def b_y(self, zr):
         self.recv(1, (zr, 1, 0, None), ("Y", zr))
         self.b_fan(zr, 1)
+        if self.y_first:
+            self.b_up(1)
+        else:
+            self.b_p(zr)
+
+    def b_p(self, zr):
         self.sib(1, zr, 0)
 
     def b_r(self, zr, way):
@@ -246,9 +259,9 @@
         return (wbuf.at[:, :, :, rows], wbuf.at[0:NZ - 1, :, :, rows],
                 wbuf.at[NZ - 1, 0, :, rows], wbuf.at[NZ - 1, 1, 0:NX - 1, rows])
 
-    gk = Gather(DIRECT[0], RELAY[0], me, k_s, k_r, ks_r, *rows_of(kbuf))
-    gq = Gather(DIRECT[1], RELAY[1], me, q_s, q_r, qs_r, *rows_of(qbuf))
-    gw = Gather(DIRECT[2], RELAY[2], me, w_s, w_r, ws_r, w_slot, w_most)
+    gk = Gather(DIRECT[0], RELAY[0], Y_FIRST[0], me, k_s, k_r, ks_r, *rows_of(kbuf))
+    gq = Gather(DIRECT[1], RELAY[1], Y_FIRST[1], me, q_s, q_r, qs_r, *rows_of(qbuf))
+    gw = Gather(DIRECT[2], RELAY[2], Y_FIRST[2], me, w_s, w_r, ws_r, w_slot, w_most)
 
     def both(first, second):
         pl.when(c == 0)(first)

time: 74.2 us -> 73.8 us (level)
  no operation moved by 1% of the time
where the time goes in v5:
time: 73.8 us; the launch traced here: 73.6 us
  Pallas kernels  69.8 us (95%)
  local copies, waits for them, and re-layouts  2.92 us (4%)
  other arithmetic  0.89 us (1%)
    pallas_call x1, Pallas kernels, on_device(): pl.pallas_call(kernel, out_shape=jax.ShapeDtypeStruct((rows, D), bf16), i...  69.8 us
    unnamed x3, local copies, waits for them, and re-layouts  2.92 us

profile of v5, /device:TPU:9, one launch (start us, length us, event | category | flops | bytes accessed | tf_op | source)
XLA Modules:
  0.0 73.6 jit_solution(7357498643040218240)
XLA Ops:
  0.0 0.9 %pad_maximum_fusion.packed = bf16[64,1280]{1,0:T(8,128)(2,1)S(1)} fusion(bf16[64,512]{1,0:T(8,128)(2,1)} %bitcast.3, bf16[64,512]{1,0:T(8,128)(2,1)} %param.8, bf16[64,128]{1,0:T(8,128)(2,1)} %param.10, bf16[64,128]{1,0:T(8,128)(2,1)} %param.9), kind=kLoop, calls=%fused_computation | loop fusion | flops 655360 | bytes 327680 | tf_op jit(solution)/shard_map/concatenate | solution.py:541
  0.9 0.0 copy-start
  0.9 0.9 %copy-done = s32[32768]{0:T(1024)S(1)} copy-done((s32[32768]{0:T(1024)S(1)}, s32[32768]{0:T(1024)}, u32[]{:S(2)}) %copy-start) | copy-done | bytes 131096
  1.8 69.8 %layer.1 = bf16[256,8192]{1,0:T(8,128)(2,1)S(1)} custom-call(bf16[256,8192]{1,0:T(8,128)(2,1)} %hid_hbm.1, s32[256,128]{1,0:T(8,128)S(1)} %bitcast.2, bf16[64,1280]{1,0:T(8,128)(2,1)S(1)} %pad_maximum_fusion.packed), custom_call_target="tpu_custom_call" | custom-call | tf_op jit(solution)/shard_map/layer/pallas_call | solution.py:511
  71.6 2.0 %copy.8 = bf16[256,8192]{1,0:T(8,128)(2,1)} copy(bf16[256,8192]{1,0:T(8,128)(2,1)S(1)} %layer.1) | data formatting | bytes 8388608
Async XLA Ops:
  0.9 0.9 %copy-start = (s32[32768]{0:T(1024)S(1)}, s32[32768]{0:T(1024)}, u32[]{:S(2)}) copy-start(s32[32768]{0:T(1024)} %param.7) | copy-start | bytes 393220

commit v6 on v5

--- a/solution.py
+++ b/solution.py
@@ -46,7 +46,9 @@
         (),
         (),
         (("w","d",-3),),
+        (),
         (("w","d",3),),
+        (),
         (("w","d",4),),
         (),
         (),
@@ -66,6 +68,8 @@
         (("w","d",2),),
         (("w","r",4,1),("w","r",4,-1),("w","d",-3),),
         (("w","d",3),),
+        (),
+        (),
         (("w","d",4),),
         (),
         (),
@@ -289,8 +293,8 @@
     def greet(device):
         pl.semaphore_signal(barrier, inc=1, device_id=device, device_id_type=MESH)
 
-    moves = [(0, 0, 1), (0, 0, -1), (0, 0, 2), (0, 1, 0), (0, -1, 0)]
-    moves += [(way * far, 0, 0) for far in (1, 2, 3) for way in (1, -1)]
+    moves = [(0, 0, 1), (0, 0, -1), (0, 1, 0), (0, -1, 0)]
+    moves += [(way * far, 0, 0) for far in range(1, max(DIRECT) + 1) for way in (1, -1)]
     for move in moves:
         greet(me.at(*move))
     greet(me.sibling())
@@ -435,31 +439,32 @@
             qrot[b, h] = rotated(b, h)
     run(12)
 
-    def attend(b):
+    def attend(b, first):
         window = kvw.at[b, pl.ds(c, REACH + 1)]
         span = (REACH + 1) * BLOCK
         keys = window[:, :, 0:HD].reshape(span, HD)
         values = window[:, :, HD:2 * HD].reshape(span, HD)
         scale = math.log2(math.e) / math.sqrt(HD)
-        scores = lax.dot_general(qrot[b].reshape(HQ * BLOCK, HD), keys, (((1,), (1,)), ((), ())),
+        scores = lax.dot_general(qrot[b, first:first + 2].reshape(2 * BLOCK, HD), keys, (((1,), (1,)), ((), ())),
                                  preferred_element_type=jnp.float32)
-        scores = scores.reshape(HQ, BLOCK, span) * scale + bias[b][None]
-        scores = scores.reshape(HQ * BLOCK, span)
+        scores = scores.reshape(2, BLOCK, span) * scale + bias[b][None]
+        scores = scores.reshape(2 * BLOCK, span)
         peak = jnp.max(scores, axis=1, keepdims=True)
         terms = jnp.exp2(scores - peak)
         total = jnp.sum(terms, axis=1, keepdims=True)
         result = jnp.dot(terms.astype(jnp.bfloat16), values, preferred_element_type=jnp.float32)
         result = (result * (1.0 / total)).astype(jnp.bfloat16)
-        for h in range(HQ):
-            mixed[b * BLOCK:(b + 1) * BLOCK, h * HD:(h + 1) * HD] = result[h * BLOCK:(h + 1) * BLOCK]
+        for h in range(2):
+            columns = slice((first + h) * HD, (first + h + 1) * HD)
+            mixed[b * BLOCK:(b + 1) * BLOCK, columns] = result[h * BLOCK:(h + 1) * BLOCK]
 
     for m in range(0, 5):
         pl.when(k >= m)(lambda m=m: kv_side(0, m, 1 - c).wait_recv())
         kv_side(1, m, 1 - c).wait_recv()
-    attend(0)
-
-    run(13)
-    attend(1)
+    attend(0, 0)
+    for n in range(1, 4):
+        run(12 + n)
+        attend(n // 2, 2 * (n % 2))
 
 
     def out_copy(t):
@@ -481,7 +486,7 @@
         out_copy(t).start()
 
     for n in range(3):
-        run(14 + n)
+        run(16 + n)
         pl.loop(edges[n + 1] if n else 0, edges[n + 2])(emit)
 
     def finish(core):

time: 73.8 us -> 72.8 us (0.986)
  Pallas kernels: 69.8 us -> 68.7 us
    pallas_call x1, Pallas kernels: 69.8 us -> 68.7 us  [on_device(): pl.pallas_call(kernel, out_shape=jax.ShapeDtypeStruct((rows, D), bf16), i...]
where the time goes in v6:
time: 72.8 us; the launch traced here: 72.6 us
  Pallas kernels  68.7 us (94%)
  local copies, waits for them, and re-layouts  2.92 us (4%)
  other arithmetic  0.89 us (1%)
    pallas_call x1, Pallas kernels, on_device(): pl.pallas_call(kernel, out_shape=jax.ShapeDtypeStruct((rows, D), bf16), i...  68.7 us
    unnamed x3, local copies, waits for them, and re-layouts  2.92 us

profile of v6, /device:TPU:9, one launch (start us, length us, event | category | flops | bytes accessed | tf_op | source)
XLA Modules:
  0.0 72.6 jit_solution(5914935840915673639)
XLA Ops:
  0.0 0.9 %pad_maximum_fusion.packed = bf16[64,1280]{1,0:T(8,128)(2,1)S(1)} fusion(bf16[64,512]{1,0:T(8,128)(2,1)} %bitcast.3, bf16[64,512]{1,0:T(8,128)(2,1)} %param.8, bf16[64,128]{1,0:T(8,128)(2,1)} %param.10, bf16[64,128]{1,0:T(8,128)(2,1)} %param.9), kind=kLoop, calls=%fused_computation | loop fusion | flops 655360 | bytes 327680 | tf_op jit(solution)/shard_map/concatenate | solution.py:546
  0.9 0.0 copy-start
  0.9 0.9 %copy-done = s32[32768]{0:T(1024)S(1)} copy-done((s32[32768]{0:T(1024)S(1)}, s32[32768]{0:T(1024)}, u32[]{:S(2)}) %copy-start) | copy-done | bytes 131096
  1.8 68.7 %layer.1 = bf16[256,8192]{1,0:T(8,128)(2,1)S(1)} custom-call(bf16[256,8192]{1,0:T(8,128)(2,1)} %hid_hbm.1, s32[256,128]{1,0:T(8,128)S(1)} %bitcast.2, bf16[64,1280]{1,0:T(8,128)(2,1)S(1)} %pad_maximum_fusion.packed), custom_call_target="tpu_custom_call" | custom-call | tf_op jit(solution)/shard_map/layer/pallas_call | solution.py:516
  70.5 2.0 %copy.8 = bf16[256,8192]{1,0:T(8,128)(2,1)} copy(bf16[256,8192]{1,0:T(8,128)(2,1)S(1)} %layer.1) | data formatting | bytes 8388608
Async XLA Ops:
  0.9 0.9 %copy-start = (s32[32768]{0:T(1024)S(1)}, s32[32768]{0:T(1024)}, u32[]{:S(2)}) copy-start(s32[32768]{0:T(1024)} %param.7) | copy-start | bytes 393220

commit v7 on v6

--- a/solution.py
+++ b/solution.py
@@ -397,18 +397,18 @@
     early_own, late_own = kvw.at[0, REACH + c], kvw.at[1, c]
 
     def kv_up(m):
-        return kv_copy(early_own, kvw.at[0, REACH - 2 * m + c], kv_s.at[0, m], kv_r.at[0, m], me.on(k + m, c))
+        return kv_copy(early_own, kvw.at[0, REACH - 2 * m + c], kv_s, kv_r.at[0, m], me.on(k + m, c))
 
     def kv_over(m):
-        return kv_copy(early_own, kvw.at[1, 2 * m + 1 - c], kv_s.at[0, m], kv_r.at[1, m],
+        return kv_copy(early_own, kvw.at[1, 2 * m + 1 - c], kv_s, kv_r.at[1, m],
                        me.on(2 * CHIPS - 1 - k - m, 1 - c))
 
     def kv_down(m):
-        return kv_copy(late_own, kvw.at[1, 2 * m + c], kv_s.at[1, m], kv_r.at[1, m], me.on(k - m, c))
+        return kv_copy(late_own, kvw.at[1, 2 * m + c], kv_s, kv_r.at[1, m], me.on(k - m, c))
 
     def kv_side(b, m, core):
         ref = kvw.at[0, REACH - 2 * m + core] if b == 0 else kvw.at[1, 2 * m + core]
-        return kv_copy(ref, ref, kvs_s.at[b, m], kvs_r.at[b, m], me.sibling())
+        return kv_copy(ref, ref, kvs_s, kvs_r.at[b, m], me.sibling())
 
     for m in range(4, 0, -1):
         pl.when(k + m < CHIPS)(lambda m=m: kv_up(m).start())
@@ -424,11 +424,11 @@
 
     for m in range(1, 5):
         def early_in(m=m):
-            kv_copy(early_own, kvw.at[0, REACH - 2 * m + c], kv_s.at[0, m], kv_r.at[0, m], me.sibling()).wait_recv()
+            kv_copy(early_own, kvw.at[0, REACH - 2 * m + c], kv_s, kv_r.at[0, m], me.sibling()).wait_recv()
             kv_side(0, m, c).start()
 
         pl.when(k >= m)(early_in)
-        kv_copy(late_own, kvw.at[1, 2 * m + c], kv_s.at[1, m], kv_r.at[1, m], me.sibling()).wait_recv()
+        kv_copy(late_own, kvw.at[1, 2 * m + c], kv_s, kv_r.at[1, m], me.sibling()).wait_recv()
         kv_side(1, m, c).start()
 
     run(10)
@@ -496,7 +496,7 @@
 
     both(lambda: finish(0), lambda: finish(1))
     for m in range(1, 5):
-        kv_copy(early_own, early_own, kv_s.at[0, m], kv_r.at[0, m], me.sibling()).wait_send()
+        kv_copy(early_own, early_own, kv_s, kv_r.at[0, m], me.sibling()).wait_send()
         pl.when(k >= m)(lambda m=m: kv_down(m).wait_send())
     for m in range(0, 5):
         pl.when(k >= m)(lambda m=m: kv_side(0, m, c).wait_send())
@@ -538,7 +538,7 @@
             dma, dma((40,)), dma((NZ,)),
             dma, dma((40,)), dma((NZ,)),
             dma, dma((40,)), dma((NZ,)),
-            dma((2, 5)), dma((2, 5)), dma((2, 5)), dma((2, 5)),
+            dma, dma((2, 5)), dma, dma((2, 5)),
         ],
         compiler_params=pltpu.CompilerParams(
             collective_id=1, has_side_effects=True, vmem_limit_bytes=48 * 2**20),

time: 72.8 us -> 72.6 us (level)
  no operation moved by 1% of the time
where the time goes in v7:
time: 72.6 us; the launch traced here: 72.4 us
  Pallas kernels  68.6 us (94%)
  local copies, waits for them, and re-layouts  2.92 us (4%)
  other arithmetic  0.89 us (1%)
    pallas_call x1, Pallas kernels, on_device(): pl.pallas_call(kernel, out_shape=jax.ShapeDtypeStruct((rows, D), bf16), i...  68.6 us
    unnamed x3, local copies, waits for them, and re-layouts  2.92 us

profile of v7, /device:TPU:9, one launch (start us, length us, event | category | flops | bytes accessed | tf_op | source)
XLA Modules:
  0.0 72.4 jit_solution(6330073312140356532)
XLA Ops:
  0.0 0.9 %pad_maximum_fusion.packed = bf16[64,1280]{1,0:T(8,128)(2,1)S(1)} fusion(bf16[64,512]{1,0:T(8,128)(2,1)} %bitcast.3, bf16[64,512]{1,0:T(8,128)(2,1)} %param.8, bf16[64,128]{1,0:T(8,128)(2,1)} %param.10, bf16[64,128]{1,0:T(8,128)(2,1)} %param.9), kind=kLoop, calls=%fused_computation | loop fusion | flops 655360 | bytes 327680 | tf_op jit(solution)/shard_map/concatenate | solution.py:546
  0.9 0.0 copy-start
  0.9 0.9 %copy-done = s32[32768]{0:T(1024)S(1)} copy-done((s32[32768]{0:T(1024)S(1)}, s32[32768]{0:T(1024)}, u32[]{:S(2)}) %copy-start) | copy-done | bytes 131096
  1.8 68.6 %layer.1 = bf16[256,8192]{1,0:T(8,128)(2,1)S(1)} custom-call(bf16[256,8192]{1,0:T(8,128)(2,1)} %hid_hbm.1, s32[256,128]{1,0:T(8,128)S(1)} %bitcast.2, bf16[64,1280]{1,0:T(8,128)(2,1)S(1)} %pad_maximum_fusion.packed), custom_call_target="tpu_custom_call" | custom-call | tf_op jit(solution)/shard_map/layer/pallas_call | solution.py:516
  70.4 2.0 %copy.8 = bf16[256,8192]{1,0:T(8,128)(2,1)} copy(bf16[256,8192]{1,0:T(8,128)(2,1)S(1)} %layer.1) | data formatting | bytes 8388608
Async XLA Ops:
  0.9 0.9 %copy-start = (s32[32768]{0:T(1024)S(1)}, s32[32768]{0:T(1024)}, u32[]{:S(2)}) copy-start(s32[32768]{0:T(1024)} %param.7) | copy-start | bytes 393220
